TPU v7x, 32 devices: a whole 2x2x4 slice. The times are simulated.
32 devices in a mesh: dp: 4 (over y, x), tensor: 8 (over z, core).
Axes of the slice: x: 2, y: 2, z: 4, core: 2. Of those that a mesh axis runs over, the one named last changes fastest.
Arguments:
- tokens: bfloat16 [2048, 2048], P(('dp', 'tensor')), may hold values from -40 to 40
- attn_gain: bfloat16 [2048], replicated, may hold values from 0.099609375 to 1.8984375
- moe_gain: bfloat16 [2048], replicated, may hold values from 0.099609375 to 1.8984375
- q_gain: bfloat16 [128], replicated, may hold values from 0.099609375 to 1.8984375
- k_gain: bfloat16 [128], replicated, may hold values from 0.099609375 to 1.8984375
- query_weight: bfloat16 [2048, 4096], P(None, 'tensor'), may hold values from -0.125 to 0.125
- w_kv: bfloat16 [256, 4, 2048], P('tensor'), may hold values from -0.125 to 0.125
- w_o: bfloat16 [4096, 2048], P('tensor'), may hold values from -0.5 to 0.5
- w_gate: bfloat16 [64, 768, 2048], P('tensor'), may hold values from -0.125 to 0.125
- w_up: bfloat16 [64, 768, 2048], P('tensor'), may hold values from -0.125 to 0.125
- w_down: bfloat16 [64, 768, 2048], P('tensor'), may hold values from -0.21875 to 0.21875
- shrink_qkv: bfloat16 [16, 48, 2048], P('dp'), may hold values from -0.125 to 0.125
- shrink_o: bfloat16 [16, 16, 4096], P(None, None, 'tensor'), may hold values from -0.5 to 0.5
- query_up_factors: bfloat16 [16, 16, 4096], P(None, None, 'tensor'), may hold values from -1.5 to 1.5
- key_value_up_factors: bfloat16 [16, 16, 1024], replicated, may hold values from -1.5 to 1.5
- expand_o: bfloat16 [16, 16, 2048], replicated, may hold values from -1.5 to 1.5
- lengths: int32 [4, 32], P('dp'), may hold values from 1 to 256, 512 in all within a row
- groups: int32 [4, 32], P('dp'), may hold values from 0 to 3, never falling along the last dimension, each value on 1 to 16 neighbouring positions
- adapter_of_request: int32 [4, 32], P('dp'), may hold values from 0 to 15
- adapter_slot: int32 [16], replicated, may hold values from 0 to 15, each once
- page_table: int32 [4, 64], P('dp'), may hold values from 0 to 63, each once within a row
- expert_ids: int32 [2048, 8], P('dp'), may hold values from 0 to 63, all different within a row; in each aligned block of 64 rows (0 to 63, 64 to 127, ...) at most 16 rows name the same one
- expert_gates: float32 [2048, 8], P('dp'), may hold values from 0.05 to 1
Outputs:
- attn_out: bfloat16 [2048, 2048], P(('dp', 'tensor'))
- moe_out: bfloat16 [2048, 2048], P(('dp', 'tensor'))
- kv_pages: bfloat16 [256, 1024, 128], P('dp', 'tensor')
Inputs may be any that keep to these rules, and one draw needn't show every extreme that they name: `lengths`: each row sums to 512; its largest entry is exactly 256. `groups`: never falling along a row; each group holds 1 to 16 consecutive requests, one exactly 16. `adapter_slot`: A permutation; the factors of slots k * 16 / 4 to (k + 1) * 16 / 4 - 1 are held at dp index k. `page_table`: each row is a permutation of the pages of that token group's pool. `expert_ids`: A token's 8 experts are distinct; within each aligned block of 64 rows (the rows of one device) no expert is chosen by more than 16 tokens, a bound that some block reaches.
All inputs are finite; a program needn't handle non-finite values.
Results may differ from a plain program's by a relative error of at most 0.025.
Values may be sent and summed in bfloat16 or wider, within the bound.
No kernel may reach another device: no remote copies, remote signals or barrier semaphores. Data moves between devices by JAX's collectives and lax.ppermute only.
A program may use at most 192 MiB of HBM per device.

v0:
```python
import functools
import math

import jax
import jax.numpy as jnp
from jax import lax
from jax.experimental import pallas as pl
from jax.experimental.pallas import tpu as pltpu
from jax.sharding import PartitionSpec as P

PAGE = 128
CAP_DEV = 16
NORM_EPS = 1e-06
ROPE_BASE = 1000000.0
ADAPTER_FACTOR = 0.5
MIB = 1 << 20
BF16 = jnp.bfloat16
F32 = jnp.float32
VMEM = pl.BlockSpec(memory_space=pltpu.VMEM)
SMEM = pl.BlockSpec(memory_space=pltpu.SMEM)
ANY = pl.BlockSpec(memory_space=pl.ANY)
HBM = pl.BlockSpec(memory_space=pltpu.HBM)


def dot(a, b):
    return jnp.dot(a, b, preferred_element_type=F32)


def dot_nt(a, b):
    return lax.dot_general(a, b, (((1,), (1,)), ((), ())), preferred_element_type=F32)


def lookup(index_value, table):
    match = index_value[:, None] == jnp.arange(table.shape[0], dtype=jnp.int32)[None, :]
    return jnp.sum(jnp.where(match, table[None, :], 0), axis=1)


def loop(count, body, carry):
    if count <= 2:
        for i in range(count):
            carry = body(i, carry)
        return carry
    return lax.fori_loop(0, count, body, carry)


def rms(v, gain):
    return v * lax.rsqrt(jnp.mean(v * v, axis=-1, keepdims=True) + NORM_EPS) * gain


def total_of(parts):
    total = parts[0][...].astype(F32)
    for part in parts[1:]:
        total = total + part[...].astype(F32)
    return total


def residual_kernel(count, x_ref, gain_ref, *refs):
    attn_ref, out_ref = refs[-2:]
    total = jnp.concatenate([total_of(refs[:count]), total_of(refs[count:-2])], axis=1)
    attn_ref[...] = total.astype(BF16)
    out_ref[...] = rms(x_ref[...].astype(F32) + total, gain_ref[...].astype(F32)).astype(BF16)


def residual_norm(x, gain, left, right):
    shape = jax.ShapeDtypeStruct(x.shape, BF16)
    return pl.pallas_call(
        functools.partial(residual_kernel, len(left)),
        out_shape=(shape, shape),
        in_specs=[VMEM] * (2 + len(left) + len(right)),
        out_specs=(VMEM, VMEM),
        name="residual_norm",
    )(x, gain.reshape(1, -1), *left, *right)


def total_kernel(count, *refs):
    out_ref = refs[-1]
    half = out_ref.shape[1] // 2
    out_ref[:, :half] = total_of(refs[:count]).astype(BF16)
    out_ref[:, half:] = total_of(refs[count:-1]).astype(BF16)


def total_rows(left, right):
    rows, half = left[0].shape
    return pl.pallas_call(
        functools.partial(total_kernel, len(left)),
        out_shape=jax.ShapeDtypeStruct((rows, 2 * half), BF16),
        in_specs=[VMEM] * (len(left) + len(right)),
        out_specs=VMEM,
        name="total_rows",
    )(*left, *right)


def hold_kernel(source_ref, out_ref, sem):
    copy = pltpu.make_async_copy(source_ref, out_ref, sem)
    copy.start()
    copy.wait()


def hold(rows):
    return pl.pallas_call(
        hold_kernel,
        out_shape=pltpu.VMEM(rows.shape, BF16),
        in_specs=[HBM],
        out_specs=VMEM,
        scratch_shapes=[pltpu.SemaphoreType.DMA],
        compiler_params=pltpu.CompilerParams(vmem_limit_bytes=4 * MIB),
        name="hold",
    )(pltpu.with_memory_space_constraint(rows, pltpu.HBM))


def pair_kernel(a_ref, b_ref, *outs):
    rows, half = outs[0].shape
    for i in range(len(outs) // 2):
        here = slice(i * rows, (i + 1) * rows)
        total = (a_ref[here, :].astype(F32) + b_ref[here, :].astype(F32)).astype(BF16)
        outs[2 * i][...] = total[:, :half]
        outs[2 * i + 1][...] = total[:, half:]


def pair_sum(a, b, count):
    shape = jax.ShapeDtypeStruct((a.shape[0] // count, a.shape[1] // 2), BF16)
    return pl.pallas_call(
        pair_kernel,
        out_shape=(shape,) * (2 * count),
        in_specs=[VMEM, VMEM],
        out_specs=(VMEM,) * (2 * count),
        compiler_params=pltpu.CompilerParams(vmem_limit_bytes=24 * MIB),
        name="pair_sum",
    )(a, b)


def attention_kernel(
    token_blocks,
    factor_blocks,
    head_blocks,
    spot_ref,
    gain_ref,
    row_ref,
    colslot_ref,
    oslot_ref,
    cos_ref,
    sin_ref,
    qg_ref,
    kg_ref,
    sho_ref,
    *refs,
):
    (wq_source, up_source, wo_source, exo_source), refs = refs[:4], refs[4:]
    tokens, refs = refs[:token_blocks], refs[token_blocks:]
    pieces, refs = refs[:factor_blocks], refs[factor_blocks:]
    parts, refs = refs[:head_blocks], refs[head_blocks:]
    own_ref, part_ref, kv_ref = refs[:3]
    wq_ref, up_ref, wo_ref, exo_ref, x_ref, s_ref, w_ref, qf_ref, kvf_ref, q_ref = refs[3:13]
    meta_ref, x_sems, s_sems, w_sems = refs[13:]
    meta_ref[...] = row_ref[...].T
    rows, width = x_ref.shape
    query_cols = wq_ref.shape[1]
    head = qg_ref.shape[1]
    heads = query_cols // head
    block = min(256, rows // 2)
    blocks = rows // block
    scale = head**-0.5
    devices, cols, _ = w_ref.shape
    chips = devices // 2
    own_rows = rows // devices
    chip, core = spot_ref[0], spot_ref[1]
    token_copies, factor_copies, head_copies = [], [], []
    for i, piece in enumerate(tokens):
        target = x_ref.at[pl.ds(i * own_rows, own_rows)]
        token_copies.append(pltpu.make_async_copy(piece, target, x_sems.at[i]))
        token_copies[-1].start()
    for q in range(2):
        for j in range(chips):
            device = (chip ^ j) * 2 + (core ^ q)
            head_copies.append(
                pltpu.make_async_copy(
                    parts[q].at[j], w_ref.at[device], w_sems.at[q * chips + j]
                )
            )
            head_copies[-1].start()
    token_copies.append(pltpu.make_async_copy(wq_source, wq_ref, x_sems.at[devices]))
    token_copies[-1].start()
    factor_copies.append(pltpu.make_async_copy(up_source, up_ref, x_sems.at[devices + 1]))
    factor_copies[-1].start()
    for i, piece in enumerate(pieces):
        target = s_ref.at[pl.ds(spot_ref[2 + i], piece.shape[0])]
        factor_copies.append(pltpu.make_async_copy(piece, target, s_sems.at[i]))
        factor_copies[-1].start()
    last_copies = [
        pltpu.make_async_copy(wo_source, wo_ref, x_sems.at[devices + 2]),
        pltpu.make_async_copy(exo_source, exo_ref, x_sems.at[devices + 3]),
    ]
    for copy in last_copies:
        copy.start()
    factors = s_ref.shape[0] * s_ref.shape[1]
    gain = gain_ref[...].astype(F32)
    qg = qg_ref[...].astype(F32)
    kg = kg_ref[...].astype(F32)

    for copy in token_copies + head_copies:
        copy.wait()

    def project(i, carry):
        here = pl.ds(pl.multiple_of(i * block, block), block)
        x = rms(x_ref[here, :].astype(F32), gain).astype(BF16)
        x_ref[here, :] = x
        qf_ref[here, :] = dot(x, wq_ref[...])
        kvf_ref[here, :] = dot_nt(x, w_ref[...].reshape(devices * cols, width))
        return carry

    loop(blocks, project, 0)

    for copy in factor_copies:
        copy.wait()

    def turned(v, gain, here):
        v = rms(v, gain)
        return v * cos_ref[here, :] + pltpu.roll(v, head // 2, 1) * sin_ref[here, :]

    def adapt(i, carry):
        here = pl.ds(pl.multiple_of(i * block, block), block)
        low = dot_nt(x_ref[here, :], s_ref[...].reshape(factors, width))
        low = jnp.where(meta_ref[here, 0:1] == colslot_ref[...], low, 0.0).astype(BF16)
        delta = ADAPTER_FACTOR * dot(low, up_ref[...])
        q = qf_ref[here, :] + delta[:, :query_cols]
        kv = (kvf_ref[here, :] + delta[:, query_cols:]).astype(BF16)
        for h in range(heads):
            cut = slice(h * head, (h + 1) * head)
            q_ref[here, cut] = turned(q[:, cut], qg, here).astype(BF16)
        kv_ref[here, :head] = turned(kv[:, :head].astype(F32), kg, here).astype(BF16)
        kv_ref[here, head:] = kv[:, head:]
        return carry

    loop(blocks, adapt, 0)

    for copy in last_copies:
        copy.wait()

    def attend(target, offset):
        def one(i, carry):
            there = pl.ds(pl.multiple_of(i * block, block), block)
            here = pl.ds(pl.multiple_of(offset + i * block, block), block)
            allowed = (row_ref[2:3, :] <= meta_ref[here, 2:3]) & (
                row_ref[1:2, :] == meta_ref[here, 1:2]
            )
            heads_mixed = []
            for h in range(heads):
                cut = slice(h * head, (h + 1) * head)
                s = dot_nt(q_ref[here, cut], kv_ref[:, :head]) * scale
                raised = jnp.where(allowed, jnp.exp(s), 0.0)
                mixed = dot(raised.astype(BF16), kv_ref[:, head:])
                mixed = mixed / jnp.sum(raised, axis=1, keepdims=True)
                heads_mixed.append(mixed.astype(BF16))
            mixed = jnp.concatenate(heads_mixed, axis=1)
            low = dot_nt(mixed, sho_ref[...])
            low = jnp.where(meta_ref[here, 0:1] == oslot_ref[...], low, 0.0).astype(BF16)
            step = min(512, width)
            for c in range(0, width, step):
                cut = slice(c, c + step)
                term = dot(mixed, wo_ref[:, cut]) + ADAPTER_FACTOR * dot(low, exo_ref[:, cut])
                target[there, cut] = term.astype(BF16)
            return carry

        loop(blocks // 2, one, 0)

    attend(part_ref, rows // 2)
    attend(own_ref, 0)


def attention(spots, tokens, weights, meta, pieces, parts, adapters):
    gain, wq, up, qg, kg, sho, wo, exo = weights
    own_rows, width = tokens[0].shape
    rows = own_rows * len(tokens)
    chips, cols, _ = parts[0].shape
    query_cols = wq.shape[1]
    head = qg.shape[1]
    ranks = pieces[0].shape[1]
    half = jax.ShapeDtypeStruct((rows // 2, width), BF16)
    flops = 2 * rows * (width * (adapters * ranks + 2 * query_cols + 2 * head) + rows * query_cols)
    return pl.pallas_call(
        functools.partial(attention_kernel, len(tokens), len(pieces), len(parts)),
        out_shape=(half, half, jax.ShapeDtypeStruct((rows, 2 * head), BF16)),
        in_specs=[SMEM] + [VMEM] * 9 + [ANY] * (4 + len(tokens) + len(pieces) + len(parts)),
        out_specs=(VMEM, VMEM, VMEM),
        scratch_shapes=[
            pltpu.VMEM(wq.shape, BF16),
            pltpu.VMEM(up.shape, BF16),
            pltpu.VMEM(wo.shape, BF16),
            pltpu.VMEM(exo.shape, BF16),
            pltpu.VMEM((rows, width), BF16),
            pltpu.VMEM((adapters, ranks, width), BF16),
            pltpu.VMEM((2 * chips, cols, width), BF16),
            pltpu.VMEM((rows, query_cols), F32),
            pltpu.VMEM((rows, 2 * head), F32),
            pltpu.VMEM((rows, query_cols), BF16),
            pltpu.VMEM((rows, meta[0].shape[0]), F32),
            pltpu.SemaphoreType.DMA((2 * chips + 4,)),
            pltpu.SemaphoreType.DMA((len(pieces),)),
            pltpu.SemaphoreType.DMA((2 * chips,)),
        ],
        compiler_params=pltpu.CompilerParams(vmem_limit_bytes=60 * MIB),
        cost_estimate=pl.CostEstimate(
            flops=flops, bytes_accessed=16 * MIB, transcendentals=rows * rows
        ),
        name="attention",
    )(spots, gain, *meta, qg, kg, sho, wq, up, wo, exo, *tokens, *pieces, *parts)


def pages_kernel(first_ref, length_ref, page_ref, entries_ref, out_ref):
    columns, extent = entries_ref.shape
    rows = extent - PAGE
    window = 2 * PAGE
    gap = lax.broadcasted_iota(jnp.int32, (window, PAGE), 0) - lax.broadcasted_iota(
        jnp.int32, (window, PAGE), 1
    )
    lane = lax.broadcasted_iota(jnp.int32, (columns, PAGE), 1)

    def one(n, carry):
        length = length_ref[n]
        page = page_ref[n]

        @pl.when(length > 0)
        def _():
            first = jnp.minimum(first_ref[n], rows - 1)
            base = pl.multiple_of(first // PAGE * PAGE, PAGE)
            pick = (gap == first - base).astype(F32).astype(BF16)
            moved = dot(entries_ref[:, pl.ds(base, window)], pick)
            out_ref[page] = jnp.where(lane < length, moved, 0.0).astype(BF16)

        @pl.when(length <= 0)
        def _():
            out_ref[page] = jnp.zeros((columns, PAGE), BF16)

        return carry

    lax.fori_loop(0, page_ref.shape[0], one, 0)


def fill_pages(first, length, page, entries):
    rows, columns = entries.shape
    count = page.shape[0]
    turned = jnp.pad(entries.T, ((0, 0), (0, PAGE)))
    return pl.pallas_call(
        pages_kernel,
        out_shape=jax.ShapeDtypeStruct((count, columns, PAGE), BF16),
        in_specs=[SMEM, SMEM, SMEM, VMEM],
        out_specs=VMEM,
        compiler_params=pltpu.CompilerParams(vmem_limit_bytes=32 * MIB),
        cost_estimate=pl.CostEstimate(
            flops=count * columns * PAGE * PAGE * 16, bytes_accessed=4 * MIB, transcendentals=0
        ),
        name="fill_pages",
    )(first, length, page, turned)


def start_all(copies):
    for copy in copies:
        copy.start()
    return copies


def wait_all(copies):
    for copy in copies:
        copy.wait()


def token_copies(pieces, x_ref, sems):
    rows = pieces[0].shape[0]
    return [
        pltpu.make_async_copy(piece, x_ref.at[pl.ds(i * rows, rows)], sems.at[i])
        for i, piece in enumerate(pieces)
    ]


def pick_rows(route_ref, x_ref, rows_ref, experts, pair, room, capacity):
    total, width = x_ref.shape
    step = min(512, width)
    line = lax.broadcasted_iota(jnp.int32, (room, pair), 0).astype(F32)
    for b in range(total // pair):
        there = slice(b * pair, (b + 1) * pair)
        pick = jnp.concatenate(
            [
                (route_ref[n : n + 1, there] == line + b * room).astype(F32).astype(BF16)
                for n in range(experts)
            ],
            axis=0,
        )
        for c in range(0, width, step):
            cut = slice(c, c + step)
            got = dot(pick, x_ref[there, cut]).astype(BF16)
            for n in range(experts):
                begin = n * capacity + b * room
                rows_ref[begin : begin + room, cut] = got[n * room : (n + 1) * room]


def combine(turned_ref, y_ref, own_ref, part_ref, experts, pair, room, capacity):
    total, width = turned_ref.shape[0], y_ref.shape[1]
    step = min(512, width)
    half = total // 2
    line = lax.broadcasted_iota(jnp.int32, (pair, experts * room), 1).astype(F32)
    for b in range(total // pair):
        here = slice(b * pair, (b + 1) * pair)
        spread = jnp.zeros((pair, experts * room), F32)
        for n in range(experts):
            place = turned_ref[here, n : n + 1] + (n - b) * room
            share = turned_ref[here, experts + n : experts + n + 1]
            spread = jnp.where(place == line, share, spread)
        spread = spread.astype(BF16)
        target, first = (own_ref, b * pair) if b * pair < half else (part_ref, b * pair - half)
        for c in range(0, width, step):
            cut = slice(c, c + step)
            begins = [n * capacity + b * room for n in range(experts)]
            y = jnp.concatenate([y_ref[begin : begin + room, cut] for begin in begins], axis=0)
            target[first : first + pair, cut] = dot(spread, y).astype(BF16)


def experts_kernel(blocks, capacity, route_ref, *refs):
    pieces, refs = refs[:blocks], refs[blocks:]
    gate_ref, up_ref, down_ref, own_ref, part_ref = refs[:5]
    x_ref, rows_ref, y_ref, turned_ref, gate_buf, up_buf, down_buf, x_sems, w_sems = refs[5:]
    experts = rows_ref.shape[0] // capacity
    slots = gate_buf.shape[0]
    streams = ((gate_ref, gate_buf), (up_ref, up_buf), (down_ref, down_buf))

    def copy(k, e, s):
        source, buffer = streams[k]
        return pltpu.make_async_copy(source.at[e], buffer.at[s], w_sems.at[k, s])

    tokens = start_all(token_copies(pieces, x_ref, x_sems))
    for e in range(min(slots, experts)):
        for k in range(3):
            copy(k, e, e).start()
    turned_ref[...] = route_ref[...].T
    wait_all(tokens)
    pair = 2 * x_ref.shape[0] // blocks
    pick_rows(route_ref, x_ref, rows_ref, experts, pair, 2 * CAP_DEV, capacity)

    def one(e, carry):
        s = lax.rem(e, slots)
        here = pl.ds(pl.multiple_of(e * capacity, capacity), capacity)
        x = rows_ref[here, :]
        copy(0, e, s).wait()
        gate = dot_nt(x, gate_buf[s])
        copy(1, e, s).wait()
        up = dot_nt(x, up_buf[s])
        hidden = (gate / (1.0 + jnp.exp(-gate)) * up).astype(BF16)
        copy(2, e, s).wait()
        y_ref[here, :] = dot(hidden, down_buf[s]).astype(BF16)

        @pl.when(e + slots < experts)
        def _():
            for k in range(3):
                copy(k, e + slots, s).start()

        return carry

    lax.fori_loop(0, experts, one, 0)
    combine(turned_ref, y_ref, own_ref, part_ref, experts, pair, 2 * CAP_DEV, capacity)


def expert_layer(routes, pieces, gate, up, down, capacity):
    experts, hidden, width = gate.shape
    own_rows = pieces[0].shape[0]
    total = own_rows * len(pieces)
    slots = min(3 if total <= 512 else 2, experts)
    half = jax.ShapeDtypeStruct((total // 2, width), BF16)
    return pl.pallas_call(
        functools.partial(experts_kernel, len(pieces), capacity),
        out_shape=(half, half),
        in_specs=[VMEM] + [ANY] * (3 + len(pieces)),
        out_specs=(VMEM, VMEM),
        scratch_shapes=[
            pltpu.VMEM((total, width), BF16),
            pltpu.VMEM((experts * capacity, width), BF16),
            pltpu.VMEM((experts * capacity, width), BF16),
            pltpu.VMEM(routes.shape[::-1], F32),
            pltpu.VMEM((slots, hidden, width), BF16),
            pltpu.VMEM((slots, hidden, width), BF16),
            pltpu.VMEM((slots, hidden, width), BF16),
            pltpu.SemaphoreType.DMA((len(pieces),)),
            pltpu.SemaphoreType.DMA((3, slots)),
        ],
        compiler_params=pltpu.CompilerParams(vmem_limit_bytes=60 * MIB),
        cost_estimate=pl.CostEstimate(
            flops=6 * experts * capacity * hidden * width,
            bytes_accessed=6 * experts * hidden * width,
            transcendentals=experts * capacity * hidden,
        ),
        name="experts",
    )(routes, *pieces, gate, up, down)


def other_core(value, parts):
    return lax.ppermute(value, "tensor", [(i, i ^ 1) for i in range(parts)])


def swap_chips(value, parts, by):
    return lax.ppermute(value, "tensor", [(i, i ^ (2 * by)) for i in range(parts)])


def swap_holder(value, holders, by):
    return lax.ppermute(value, "dp", [(i, i ^ by) for i in range(holders)])


def gather_blocks(own, parts, between=lambda blocks: blocks):
    chips = parts // 2
    blocks = {0: own}
    bit = chips // 2
    while bit:
        for i, block in list(blocks.items()):
            if i ^ bit not in blocks:
                blocks[i ^ bit] = swap_chips(block, parts, bit)
        if bit == chips // 2:
            if 1 not in blocks:
                blocks[1] = swap_chips(own, parts, 1)
            blocks = between(blocks)
        bit //= 2
    mine = [blocks[i] for i in range(chips)]
    return mine + [other_core(block, parts) for block in mine]


def scatter_terms(own, part, parts):
    chips = parts // 2
    sums = pair_sum(hold(own), other_core(part, parts), chips)
    halves = []
    for k in range(2):
        terms = {j: [sums[2 * j + k]] for j in range(chips)}
        late, last, bit = [], None, 1
        while bit < chips:
            for j in sorted((j for j in terms if j & bit), reverse=True):
                sent = terms.pop(j)
                if len(sent) > 1:
                    sent = [sum(term.astype(F32) for term in sent).astype(BF16)]
                if j == bit and 2 * bit < chips:
                    late.append((bit, sent[0]))
                    continue
                last = sent[0]
                terms[j ^ bit].append(swap_chips(last, parts, bit))
            bit *= 2
        for bit, sent in late:
            sent, last = lax.optimization_barrier((sent, last))
            terms[0].append(swap_chips(sent, parts, bit))
        halves.append(terms[0])
    return halves


def from_here(rows, chip, core, chips):
    split = rows.reshape((chips, 2, -1) + rows.shape[1:])
    split = jnp.where(core == 0, split, split[:, ::-1])
    bit = 1
    while bit < chips:
        pairs = split.reshape((chips // (2 * bit), 2, bit) + split.shape[1:])
        split = jnp.where((chip & bit) == 0, pairs, pairs[:, ::-1]).reshape(split.shape)
        bit *= 2
    return split


def to_device(rows, chip, core, chips):
    return jnp.swapaxes(from_here(rows, chip, core, chips), 0, 1).reshape(rows.shape)


def to_group(rows, chip, core, chips):
    split = jnp.swapaxes(rows.reshape((2, chips, -1) + rows.shape[1:]), 0, 1)
    return from_here(split.reshape(rows.shape), chip, core, chips).reshape(rows.shape)


def local(
    tokens,
    attn_gain,
    moe_gain,
    q_gain,
    k_gain,
    query_weight,
    w_kv,
    w_o,
    w_gate,
    w_up,
    w_down,
    shrink_qkv,
    shrink_o,
    query_up_factors,
    key_value_up_factors,
    expand_o,
    lengths,
    groups,
    adapter_of_request,
    adapter_slot,
    page_table,
    expert_ids,
    expert_gates,
):
    parts = lax.axis_size("tensor")
    place = lax.axis_index("tensor")
    holders = lax.axis_size("dp")
    holder = lax.axis_index("dp")
    chips, chip, core = parts // 2, place // 2, place % 2
    own_rows, width = tokens.shape
    total = own_rows * parts
    head_length = q_gain.shape[0]
    adapters, rank, kv_width = key_value_up_factors.shape
    kv_heads = kv_width // (2 * head_length)
    held, ranks = shrink_qkv.shape[:2]
    head = place * kv_heads // parts
    query_cols = query_weight.shape[1]
    experts = w_gate.shape[0]

    line = jnp.arange(total, dtype=jnp.int32)
    side, number = line // (total // 2), line // own_rows % chips
    position = ((number ^ chip) * 2 + (side ^ core)) * own_rows + line % own_rows
    length_row, group_row, adapter_row = lengths[0], groups[0], adapter_of_request[0]
    ends = jnp.cumsum(length_row)
    starts = ends - length_row
    request = jnp.sum((ends[None, :] <= position[:, None]).astype(jnp.int32), axis=1)
    same = group_row[:, None] == group_row[None, :]
    group_first = jnp.min(jnp.where(same, starts[None, :], total), axis=1)
    slot_of_request = lookup(adapter_row, adapter_slot)
    group = lookup(request, group_row)
    rope_pos = position - lookup(request, group_first)
    slot = lookup(request, slot_of_request)
    meta_row = jnp.stack([slot, group, position] + [position] * 5, axis=0).astype(F32)
    freq = jnp.exp(
        -jnp.arange(head_length // 2, dtype=F32) * (2.0 * math.log(ROPE_BASE) / head_length)
    )
    angle = rope_pos.astype(F32)[:, None] * freq[None, :]
    cosine, sine = jnp.cos(angle), jnp.sin(angle)
    cosine = jnp.concatenate([cosine, cosine], axis=1)
    sine = jnp.concatenate([-sine, sine], axis=1)
    colslot = (jnp.arange(adapters * ranks, dtype=jnp.int32) // ranks)[None, :].astype(F32)
    oslot = (jnp.arange(adapters * rank, dtype=jnp.int32) // rank)[None, :].astype(F32)

    up_kv = lax.dynamic_index_in_dim(
        key_value_up_factors.reshape(adapters, rank, kv_heads, 2, head_length), head, 2, keepdims=False
    )
    up = jnp.concatenate(
        [
            jnp.pad(query_up_factors, ((0, 0), (0, 2 * rank), (0, 0))),
            jnp.pad(up_kv[:, :, 0], ((0, 0), (rank, rank), (0, 0))),
            jnp.pad(up_kv[:, :, 1], ((0, 0), (2 * rank, 0), (0, 0))),
        ],
        axis=2,
    ).reshape(adapters * ranks, query_cols + 2 * head_length)

    weights = (
        attn_gain.reshape(1, -1),
        query_weight,
        up,
        q_gain.reshape(1, -1),
        k_gain.reshape(1, -1),
        shrink_o.reshape(adapters * rank, query_cols),
        w_o,
        expand_o.reshape(adapters * rank, width),
    )
    meta = (meta_row, colslot, oslot, cosine, sine)
    half = held // 2
    half_own = lax.dynamic_slice_in_dim(shrink_qkv, core * half, half, 0)
    halves = [swap_holder(half_own, holders, r) for r in range(1, holders)]
    spots = [chip, core, holder * held]
    for r in range(1, holders):
        begin = (holder ^ r) * held
        spots += [begin + core * half, begin + (1 - core) * half]
    spots = jnp.stack(spots).astype(jnp.int32)
    cuts = [
        lax.dynamic_index_in_dim(w_kv, 2 * (chip ^ j) * kv_heads // parts, 1, keepdims=False)
        for j in range(chips)
    ]

    def between(blocks):
        nonlocal cuts, meta
        blocks, halves[:2], cuts, meta = lax.optimization_barrier(
            (blocks, halves[:2], cuts, meta)
        )
        return blocks

    gathered = gather_blocks(tokens, parts, between)
    mine = [cuts[0]] + [swap_chips(cuts[j], parts, j) for j in range(1, chips)]
    mine = jnp.stack(mine)
    mine, weights, spots = lax.optimization_barrier((mine, weights, spots))
    head_parts = [mine, other_core(mine, parts)]
    pieces = [shrink_qkv]
    for got in halves:
        pieces += [got, other_core(got, parts)]
    own, part, entries = attention(
        spots,
        gathered,
        weights,
        meta,
        pieces,
        head_parts,
        adapters,
    )
    left, right = scatter_terms(own, part, parts)

    attn_own, moe_own = residual_norm(tokens, moe_gain, left, right)

    moe_own, entries, starts, length_row, page_table, expert_ids, expert_gates = (
        lax.optimization_barrier(
            (moe_own, entries, starts, length_row, page_table, expert_ids, expert_gates)
        )
    )

    local_cols = kv_width // parts
    kept = lax.dynamic_slice_in_dim(
        entries, place * local_cols - head * 2 * head_length, local_cols, 1
    )
    page_row = page_table[0]
    per_request = page_row.shape[0] // length_row.shape[0]
    offset = PAGE * jnp.arange(per_request, dtype=jnp.int32)[None, :]
    page_first = (starts[:, None] + offset).reshape(-1)
    page_length = jnp.clip(length_row[:, None] - offset, 0, PAGE).reshape(-1)
    kv_pages = fill_pages(page_first, page_length, page_row, to_group(kept, chip, core, chips))

    capacity = CAP_DEV * parts
    ids = to_device(expert_ids, chip, core, chips)
    gates = to_device(expert_gates, chip, core, chips)
    share = gates / jnp.sum(gates, axis=1, keepdims=True)
    own_experts = place * experts + jnp.arange(experts, dtype=jnp.int32)
    chosen = ids[:, :, None] == own_experts[None, None, :]
    hit = jnp.any(chosen, axis=1)
    weight = jnp.sum(jnp.where(chosen, share[:, :, None], 0.0), axis=1)
    block = line // own_rows
    earlier = (line[:, None] > line[None, :]) & (block[:, None] == block[None, :])
    before = dot(earlier.astype(BF16), hit.astype(BF16)).astype(jnp.int32)
    slot_in = jnp.where(hit, block[:, None] * CAP_DEV + before, -(1 << 20))

    routes = jnp.concatenate([slot_in.astype(F32).T, weight.T], axis=0)
    routes = jnp.pad(routes, ((0, -routes.shape[0] % 8), (0, 0)))

    def tables_first(blocks):
        nonlocal routes, kv_pages
        blocks, routes, kv_pages = lax.optimization_barrier((blocks, routes, kv_pages))
        return blocks

    gathered = gather_blocks(moe_own, parts, tables_first)
    own, part = expert_layer(routes, gathered, w_gate, w_up, w_down, capacity)
    left, right = scatter_terms(own, part, parts)

    moe_total = total_rows(left, right)
    return (attn_own, moe_total, kv_pages)


def solution(mesh):
    placed = (
        P(("dp", "tensor"), None),
        P(),
        P(),
        P(),
        P(),
        P(None, "tensor"),
        P("tensor", None, None),
        P("tensor", None),
        P("tensor", None, None),
        P("tensor", None, None),
        P("tensor", None, None),
        P("dp", None, None),
        P(None, None, "tensor"),
        P(None, None, "tensor"),
        P(),
        P(),
        P("dp", None),
        P("dp", None),
        P("dp", None),
        P(),
        P("dp", None),
        P("dp", None),
        P("dp", None),
    )
    return jax.shard_map(
        local,
        mesh=mesh,
        in_specs=placed,
        out_specs=(P(("dp", "tensor"), None), P(("dp", "tensor"), None), P("dp", "tensor", None)),
        check_vma=False,
    )
```

profile of v0, /device:TPU:0, one launch (start us, length us, event | category | flops | bytes accessed | tf_op | source)
XLA Modules:
  0.0 176.1 jit_solution(7321520518220182703)
XLA Ops:
  1.8 3.0 %collective-permute-start.2 = (bf16[2,48,2048]{2,1,0:T(8,128)(2,1)S(1)}, bf16[2,48,2048]{2,1,0:T(8,128)(2,1)S(1)}, u32[]{:S(2)}, u32[]{:S(2)}) collective-permute-start(bf16[2,48,2048]{2,1,0:T(8,128)(2,1)S(1)} %constant_dynamic-slice_fusion.6), channel_id=1, source_target_pairs={{0,8},{8,0},{16,24},{24,16},{1,9},{9,1},{17,25},{25,17},{2,10},{10... | collective-permute-start | bytes 1179656 | tf_op jit(solution)/shard_map/ppermute | solution.py:502
  4.8 1.5 collective-permute-start.3
  6.3 1.6 collective-permute-start
  7.9 2.6 %collective-permute-start.1 = (bf16[64,2048]{1,0:T(8,128)(2,1)}, bf16[64,2048]{1,0:T(8,128)(2,1)}, u32[]{:S(2)}, u32[]{:S(2)}) collective-permute-start(bf16[64,2048]{1,0:T(8,128)(2,1)} %x_ref.1), channel_id=1, source_target_pairs={{0,4},{1,5},{2,6},{3,7},{4,0},{5,1},{6,2},{7,3},{8,12},{9,13},{10,... | collective-permute-start | bytes 786440 | tf_op jit(solution)/shard_map/ppermute | solution.py:498
  23.9 1.6 collective-permute-start.4
  25.5 2.6 %collective-permute-start.5 = (bf16[32,2048]{1,0:T(8,128)(2,1)S(1)}, bf16[32,2048]{1,0:T(8,128)(2,1)S(1)}, u32[]{:S(2)}, u32[]{:S(2)}) collective-permute-start(bf16[32,2048]{1,0:T(8,128)(2,1)S(1)} %get-tuple-element.68), channel_id=1, source_target_pairs={{0,4},{1,5},{2,6},{3,7},{4,0},{5,1},{6,2},{7,3},{8,12},{9,13},{10,... | collective-permute-start | bytes 393224 | tf_op jit(solution)/shard_map/ppermute | solution.py:498
  30.1 3.2 %collective-permute-done.4 = bf16[32,2048]{1,0:T(8,128)(2,1)S(1)} collective-permute-done((bf16[32,2048]{1,0:T(8,128)(2,1)S(1)}, bf16[32,2048]{1,0:T(8,128)(2,1)S(1)}, u32[]{:S(2)}, u32[]{:S(2)}) %collective-permute-start.4) | collective-permute-done | bytes 131104 | tf_op jit(solution)/shard_map/ppermute | solution.py:498
  33.8 2.3 %collective-permute-done.6 = bf16[32,2048]{1,0:T(8,128)(2,1)S(1)} collective-permute-done((bf16[32,2048]{1,0:T(8,128)(2,1)S(1)}, bf16[32,2048]{1,0:T(8,128)(2,1)S(1)}, u32[]{:S(2)}, u32[]{:S(2)}) %collective-permute-start.6) | collective-permute-done | bytes 131104 | tf_op jit(solution)/shard_map/ppermute | solution.py:498
  36.7 2.3 %collective-permute-done.7.refs_7_ = bf16[64,2048]{1,0:T(8,128)(2,1)S(1)} collective-permute-done((bf16[64,2048]{1,0:T(8,128)(2,1)}, bf16[64,2048]{1,0:T(8,128)(2,1)S(1)}, u32[]{:S(2)}, u32[]{:S(2)}) %collective-permute-start.7) | collective-permute-done | bytes 262176 | tf_op jit(solution)/shard_map/ppermute | solution.py:498
  44.1 16.3 %attention.1 = (bf16[256,2048]{1,0:T(8,128)(2,1)}, bf16[256,2048]{1,0:T(8,128)(2,1)}, bf16[512,256]{1,0:T(8,128)(2,1)}) custom-call(s32[9]{0:T(128)} %stack.77.spot_ref, bf16[1,2048]{1,0:T(2,128)(2,1)} %reshape.389.gain_ref, f32[8,512]{1,0:T(8,128)} %convert_element_type.90.row_ref, f32[1,768]{1,0:T(1,128)} %fusion.21.colslot_ref, ...), custom_call_target="tpu_custom_call" | custom-call | flops 4563402752 | bytes 16777216 | tf_op jit(solution)/shard_map/attention/pallas_call | solution.py:280
  61.9 1.5 collective-permute-done.17.b_ref
  64.9 2.1 %collective-permute-start.18 = (bf16[64,1024]{1,0:T(8,128)(2,1)S(1)}, bf16[64,1024]{1,0:T(8,128)(2,1)S(1)}, u32[]{:S(2)}, u32[]{:S(2)}) collective-permute-start(bf16[64,1024]{1,0:T(8,128)(2,1)S(1)} %get-tuple-element.94), channel_id=1, source_target_pairs={{0,2},{1,3},{2,0},{3,1},{4,6},{5,7},{6,4},{7,5},{8,10},{9,11},{10,... | collective-permute-start | bytes 393224 | tf_op jit(solution)/shard_map/ppermute | solution.py:498
  67.0 4.2 %collective-permute-done.21 = bf16[64,1024]{1,0:T(8,128)(2,1)S(1)} collective-permute-done((bf16[64,1024]{1,0:T(8,128)(2,1)S(1)}, bf16[64,1024]{1,0:T(8,128)(2,1)S(1)}, u32[]{:S(2)}, u32[]{:S(2)}) %collective-permute-start.21) | collective-permute-done | bytes 131104 | tf_op jit(solution)/shard_map/ppermute | solution.py:498
  71.7 2.1 %collective-permute-start.23 = (bf16[64,1024]{1,0:T(8,128)(2,1)S(1)}, bf16[64,1024]{1,0:T(8,128)(2,1)S(1)}, u32[]{:S(2)}, u32[]{:S(2)}) collective-permute-start(bf16[64,1024]{1,0:T(8,128)(2,1)S(1)} %get-tuple-element.101), channel_id=1, source_target_pairs={{0,2},{1,3},{2,0},{3,1},{4,6},{5,7},{6,4},{7,5},{8,10},{9,11},{10,... | collective-permute-start | bytes 393224 | tf_op jit(solution)/shard_map/ppermute | solution.py:498
  74.4 2.0 %collective-permute-start.20 = (bf16[64,1024]{1,0:T(8,128)(2,1)S(1)}, bf16[64,1024]{1,0:T(8,128)(2,1)S(1)}, u32[]{:S(2)}, u32[]{:S(2)}) collective-permute-start(bf16[64,1024]{1,0:T(8,128)(2,1)S(1)} %get-tuple-element.96), channel_id=1, source_target_pairs={{0,2},{1,3},{2,0},{3,1},{4,6},{5,7},{6,4},{7,5},{8,10},{9,11},{10,... | collective-permute-start | bytes 393224 | tf_op jit(solution)/shard_map/ppermute | solution.py:498
  77.0 2.3 %collective-permute-done.23.refs_5_ = bf16[64,1024]{1,0:T(8,128)(2,1)S(1)} collective-permute-done((bf16[64,1024]{1,0:T(8,128)(2,1)S(1)}, bf16[64,1024]{1,0:T(8,128)(2,1)S(1)}, u32[]{:S(2)}, u32[]{:S(2)}) %collective-permute-start.23) | collective-permute-done | bytes 131104 | tf_op jit(solution)/shard_map/ppermute | solution.py:498
  79.4 2.2 %collective-permute-done.22.refs_4_ = bf16[64,1024]{1,0:T(8,128)(2,1)S(1)} collective-permute-done((bf16[64,1024]{1,0:T(8,128)(2,1)S(1)}, bf16[64,1024]{1,0:T(8,128)(2,1)S(1)}, u32[]{:S(2)}, u32[]{:S(2)}) %collective-permute-start.22) | collective-permute-done | bytes 131104 | tf_op jit(solution)/shard_map/ppermute | solution.py:498
  81.6 1.9 %collective-permute-done.20.refs_2_ = bf16[64,1024]{1,0:T(8,128)(2,1)S(1)} collective-permute-done((bf16[64,1024]{1,0:T(8,128)(2,1)S(1)}, bf16[64,1024]{1,0:T(8,128)(2,1)S(1)}, u32[]{:S(2)}, u32[]{:S(2)}) %collective-permute-start.20) | collective-permute-done | bytes 131104 | tf_op jit(solution)/shard_map/ppermute | solution.py:498
  85.3 2.2 %residual_norm.1 = (bf16[64,2048]{1,0:T(8,128)(2,1)}, bf16[64,2048]{1,0:T(8,128)(2,1)}) custom-call(bf16[64,2048]{1,0:T(8,128)(2,1)} %x_ref.1, bf16[1,2048]{1,0:T(2,128)(2,1)} %reshape.386.gain_ref, bf16[64,1024]{1,0:T(8,128)(2,1)} %copy-done, bf16[64,1024]{1,0:T(8,128)(2,1)} %copy-done.20, bf16[64,1024]{1,0:T(8,128)(2,1)} %copy-done.21, ...), custom_call_target="tpu_custom_call" | custom-call | tf_op jit(solution)/shard_map/residual_norm/pallas_call | solution.py:66
  87.8 2.3 %collective-permute-start.25 = (bf16[64,2048]{1,0:T(8,128)(2,1)}, bf16[64,2048]{1,0:T(8,128)(2,1)S(1)}, u32[]{:S(2)}, u32[]{:S(2)}) collective-permute-start(bf16[64,2048]{1,0:T(8,128)(2,1)} %get-tuple-element.113.refs_0_), channel_id=1, source_target_pairs={{0,4},{1,5},{2,6},{3,7},{4,0},{5,1},{6,2},{7,3},{8,12},{9,13},{10,... | collective-permute-start | bytes 786440 | tf_op jit(solution)/shard_map/ppermute | solution.py:498
  92.8 8.1 %fill_pages.1 = bf16[64,128,128]{2,1,0:T(8,128)(2,1)} custom-call(s32[64]{0:T(128)S(1)} %add.274.first_ref, s32[64]{0:T(128)S(1)} %min.12.length_ref, s32[64]{0:T(128)S(1)} %bitcast.85, bf16[128,640]{1,0:T(8,128)(2,1)S(1)} %pad.19.entries_ref), custom_call_target="tpu_custom_call" | custom-call | flops 2147483648 | bytes 4194304 | tf_op jit(solution)/shard_map/fill_pages/pallas_call | solution.py:343
  102.3 5.8 %collective-permute-done.26.refs_3_ = bf16[64,2048]{1,0:T(8,128)(2,1)S(1)} collective-permute-done((bf16[64,2048]{1,0:T(8,128)(2,1)S(1)}, bf16[64,2048]{1,0:T(8,128)(2,1)S(1)}, u32[]{:S(2)}, u32[]{:S(2)}) %collective-permute-start.26) | collective-permute-done | bytes 262176 | tf_op jit(solution)/shard_map/ppermute | solution.py:498
  108.2 1.5 collective-permute-done.30.refs_7_
  110.4 40.1 %experts.1 = (bf16[256,2048]{1,0:T(8,128)(2,1)}, bf16[256,2048]{1,0:T(8,128)(2,1)}) custom-call(f32[16,512]{1,0:T(8,128)} %pad_maximum_fusion.3.route_ref, bf16[64,2048]{1,0:T(8,128)(2,1)} %get-tuple-element.113.refs_0_, bf16[64,2048]{1,0:T(8,128)(2,1)} %copy-done.9, bf16[64,2048]{1,0:T(8,128)(2,1)} %copy-done.10, bf16[64,2048]{1,0:T(8,128)(2,1)} %copy-done.11, ...), custom_call_target="tpu_custom_call" | custom-call | flops 9663676416 | bytes 75497472 | tf_op jit(solution)/shard_map/experts/pallas_call | solution.py:467
  151.9 1.5 collective-permute-done.31.b_ref
  153.7 2.0 %collective-permute-start.32 = (bf16[64,1024]{1,0:T(8,128)(2,1)S(1)}, bf16[64,1024]{1,0:T(8,128)(2,1)S(1)}, u32[]{:S(2)}, u32[]{:S(2)}) collective-permute-start(bf16[64,1024]{1,0:T(8,128)(2,1)S(1)} %get-tuple-element.120), channel_id=1, source_target_pairs={{0,2},{1,3},{2,0},{3,1},{4,6},{5,7},{6,4},{7,5},{8,10},{9,11},{10,... | collective-permute-start | bytes 393224 | tf_op jit(solution)/shard_map/ppermute | solution.py:498
  155.8 4.3 %collective-permute-done.35 = bf16[64,1024]{1,0:T(8,128)(2,1)S(1)} collective-permute-done((bf16[64,1024]{1,0:T(8,128)(2,1)S(1)}, bf16[64,1024]{1,0:T(8,128)(2,1)S(1)}, u32[]{:S(2)}, u32[]{:S(2)}) %collective-permute-start.35) | collective-permute-done | bytes 131104 | tf_op jit(solution)/shard_map/ppermute | solution.py:498
  160.6 2.0 %collective-permute-start.37 = (bf16[64,1024]{1,0:T(8,128)(2,1)S(1)}, bf16[64,1024]{1,0:T(8,128)(2,1)S(1)}, u32[]{:S(2)}, u32[]{:S(2)}) collective-permute-start(bf16[64,1024]{1,0:T(8,128)(2,1)S(1)} %get-tuple-element.127), channel_id=1, source_target_pairs={{0,2},{1,3},{2,0},{3,1},{4,6},{5,7},{6,4},{7,5},{8,10},{9,11},{10,... | collective-permute-start | bytes 393224 | tf_op jit(solution)/shard_map/ppermute | solution.py:498
  162.8 2.5 %collective-permute-start.33 = (bf16[64,1024]{1,0:T(8,128)(2,1)S(1)}, bf16[64,1024]{1,0:T(8,128)(2,1)S(1)}, u32[]{:S(2)}, u32[]{:S(2)}) collective-permute-start(bf16[64,1024]{1,0:T(8,128)(2,1)S(1)} %add_convert_fusion.1), channel_id=1, source_target_pairs={{0,4},{1,5},{2,6},{3,7},{4,0},{5,1},{6,2},{7,3},{8,12},{9,13},{10,... | collective-permute-start | bytes 393224 | tf_op jit(solution)/shard_map/ppermute | solution.py:498
  165.3 6.3 %collective-permute-done.37.refs_5_ = bf16[64,1024]{1,0:T(8,128)(2,1)S(1)} collective-permute-done((bf16[64,1024]{1,0:T(8,128)(2,1)S(1)}, bf16[64,1024]{1,0:T(8,128)(2,1)S(1)}, u32[]{:S(2)}, u32[]{:S(2)}) %collective-permute-start.37) | collective-permute-done | bytes 131104 | tf_op jit(solution)/shard_map/ppermute | solution.py:498
  171.6 1.8 %collective-permute-done.34.refs_2_ = bf16[64,1024]{1,0:T(8,128)(2,1)S(1)} collective-permute-done((bf16[64,1024]{1,0:T(8,128)(2,1)S(1)}, bf16[64,1024]{1,0:T(8,128)(2,1)S(1)}, u32[]{:S(2)}, u32[]{:S(2)}) %collective-permute-start.34) | collective-permute-done | bytes 131104 | tf_op jit(solution)/shard_map/ppermute | solution.py:498
  174.1 2.0 %total_rows.1 = bf16[64,2048]{1,0:T(8,128)(2,1)} custom-call(bf16[64,1024]{1,0:T(8,128)(2,1)} %copy-done.2, bf16[64,1024]{1,0:T(8,128)(2,1)} %copy-done.25, bf16[64,1024]{1,0:T(8,128)(2,1)} %copy-done.24, bf16[64,1024]{1,0:T(8,128)(2,1)} %copy-done.3, bf16[64,1024]{1,0:T(8,128)(2,1)} %copy-done.22, bf16[64,1024]{1,0:T(8,128)(2,1)} %copy-done.23), custom_call_target="tpu_custom_call" | custom-call | tf_op jit(solution)/shard_map/total_rows/pallas_call | solution.py:84
  (210 shorter events, 37.3 us)
Async XLA Ops:
  1.8 21.0 %collective-permute-start.2 = (bf16[2,48,2048]{2,1,0:T(8,128)(2,1)S(1)}, bf16[2,48,2048]{2,1,0:T(8,128)(2,1)S(1)}, u32[]{:S(2)}, u32[]{:S(2)}) collective-permute-start(bf16[2,48,2048]{2,1,0:T(8,128)(2,1)S(1)} %constant_dynamic-slice_fusion.6), channel_id=1, source_target_pairs={{0,8},{8,0},{16,24},{24,16},{1,9},{9,1},{17,25},{25,17},{2,10},{10... | collective-permute-start | bytes 1179656 | tf_op jit(solution)/shard_map/ppermute | solution.py:502
  4.8 19.1 %collective-permute-start.3 = (bf16[2,48,2048]{2,1,0:T(8,128)(2,1)S(1)}, bf16[2,48,2048]{2,1,0:T(8,128)(2,1)}, u32[]{:S(2)}, u32[]{:S(2)}) collective-permute-start(bf16[2,48,2048]{2,1,0:T(8,128)(2,1)S(1)} %constant_dynamic-slice_fusion.6), channel_id=1, source_target_pairs={{0,16},{8,24},{16,0},{24,8},{1,17},{9,25},{17,1},{25,9},{2,18},{10... | collective-permute-start | bytes 1179656 | tf_op jit(solution)/shard_map/ppermute | solution.py:502
  6.3 16.4 %collective-permute-start = (bf16[64,2048]{1,0:T(8,128)(2,1)}, bf16[64,2048]{1,0:T(8,128)(2,1)}, u32[]{:S(2)}, u32[]{:S(2)}) collective-permute-start(bf16[64,2048]{1,0:T(8,128)(2,1)} %x_ref.1), channel_id=1, source_target_pairs={{0,2},{1,3},{2,0},{3,1},{4,6},{5,7},{6,4},{7,5},{8,10},{9,11},{10,... | collective-permute-start | bytes 786440 | tf_op jit(solution)/shard_map/ppermute | solution.py:498
  7.9 14.9 %collective-permute-start.1 = (bf16[64,2048]{1,0:T(8,128)(2,1)}, bf16[64,2048]{1,0:T(8,128)(2,1)}, u32[]{:S(2)}, u32[]{:S(2)}) collective-permute-start(bf16[64,2048]{1,0:T(8,128)(2,1)} %x_ref.1), channel_id=1, source_target_pairs={{0,4},{1,5},{2,6},{3,7},{4,0},{5,1},{6,2},{7,3},{8,12},{9,13},{10,... | collective-permute-start | bytes 786440 | tf_op jit(solution)/shard_map/ppermute | solution.py:498
  10.5 25.7 %collective-permute-start.14 = (bf16[2,48,2048]{2,1,0:T(8,128)(2,1)S(1)}, bf16[2,48,2048]{2,1,0:T(8,128)(2,1)}, u32[]{:S(2)}, u32[]{:S(2)}) collective-permute-start(bf16[2,48,2048]{2,1,0:T(8,128)(2,1)S(1)} %constant_dynamic-slice_fusion.6), channel_id=1, source_target_pairs={{0,24},{8,16},{16,8},{24,0},{1,25},{9,17},{17,9},{25,1},{2,26},{10... | collective-permute-start | bytes 1179656 | tf_op jit(solution)/shard_map/ppermute | solution.py:502
  23.9 9.4 %collective-permute-start.4 = (bf16[32,2048]{1,0:T(8,128)(2,1)S(1)}, bf16[32,2048]{1,0:T(8,128)(2,1)S(1)}, u32[]{:S(2)}, u32[]{:S(2)}) collective-permute-start(bf16[32,2048]{1,0:T(8,128)(2,1)S(1)} %get-tuple-element.67), channel_id=1, source_target_pairs={{0,2},{1,3},{2,0},{3,1},{4,6},{5,7},{6,4},{7,5},{8,10},{9,11},{10,... | collective-permute-start | bytes 393224 | tf_op jit(solution)/shard_map/ppermute | solution.py:498
  25.5 7.8 %collective-permute-start.5 = (bf16[32,2048]{1,0:T(8,128)(2,1)S(1)}, bf16[32,2048]{1,0:T(8,128)(2,1)S(1)}, u32[]{:S(2)}, u32[]{:S(2)}) collective-permute-start(bf16[32,2048]{1,0:T(8,128)(2,1)S(1)} %get-tuple-element.68), channel_id=1, source_target_pairs={{0,4},{1,5},{2,6},{3,7},{4,0},{5,1},{6,2},{7,3},{8,12},{9,13},{10,... | collective-permute-start | bytes 393224 | tf_op jit(solution)/shard_map/ppermute | solution.py:498
  28.1 8.0 %collective-permute-start.6 = (bf16[32,2048]{1,0:T(8,128)(2,1)S(1)}, bf16[32,2048]{1,0:T(8,128)(2,1)S(1)}, u32[]{:S(2)}, u32[]{:S(2)}) collective-permute-start(bf16[32,2048]{1,0:T(8,128)(2,1)S(1)} %get-tuple-element.69), channel_id=1, source_target_pairs={{0,6},{1,7},{2,4},{3,5},{4,2},{5,3},{6,0},{7,1},{8,14},{9,15},{10,... | collective-permute-start | bytes 393224 | tf_op jit(solution)/shard_map/ppermute | solution.py:498
  29.4 9.7 %collective-permute-start.7 = (bf16[64,2048]{1,0:T(8,128)(2,1)}, bf16[64,2048]{1,0:T(8,128)(2,1)S(1)}, u32[]{:S(2)}, u32[]{:S(2)}) collective-permute-start(bf16[64,2048]{1,0:T(8,128)(2,1)} %collective-permute-done.1.refs_6_), channel_id=1, source_target_pairs={{0,2},{1,3},{2,0},{3,1},{4,6},{5,7},{6,4},{7,5},{8,10},{9,11},{10,... | collective-permute-start | bytes 786440 | tf_op jit(solution)/shard_map/ppermute | solution.py:498
  33.3 5.8 %collective-permute-start.10 = (bf16[64,2048]{1,0:T(8,128)(2,1)}, bf16[64,2048]{1,0:T(8,128)(2,1)S(1)}, u32[]{:S(2)}, u32[]{:S(2)}) collective-permute-start(bf16[64,2048]{1,0:T(8,128)(2,1)} %collective-permute-done.1.refs_6_), channel_id=1, source_target_pairs={{0,1},{1,0},{2,3},{3,2},{4,5},{5,4},{6,7},{7,6},{8,9},{9,8},{10,11... | collective-permute-start | bytes 786440 | tf_op jit(solution)/shard_map/ppermute | solution.py:494
  33.3 6.3 %collective-permute-start.8 = (bf16[64,2048]{1,0:T(8,128)(2,1)S(1)}, bf16[64,2048]{1,0:T(8,128)(2,1)S(1)}, u32[]{:S(2)}, u32[]{:S(2)}) collective-permute-start(bf16[64,2048]{1,0:T(8,128)(2,1)S(1)} %copy-done.17), channel_id=1, source_target_pairs={{0,1},{1,0},{2,3},{3,2},{4,5},{5,4},{6,7},{7,6},{8,9},{9,8},{10,11... | collective-permute-start | bytes 786440 | tf_op jit(solution)/shard_map/ppermute | solution.py:494
  36.1 3.6 %collective-permute-start.9 = (bf16[64,2048]{1,0:T(8,128)(2,1)}, bf16[64,2048]{1,0:T(8,128)(2,1)S(1)}, u32[]{:S(2)}, u32[]{:S(2)}) collective-permute-start(bf16[64,2048]{1,0:T(8,128)(2,1)} %collective-permute-done.refs_5_), channel_id=1, source_target_pairs={{0,1},{1,0},{2,3},{3,2},{4,5},{5,4},{6,7},{7,6},{8,9},{9,8},{10,11... | collective-permute-start | bytes 786440 | tf_op jit(solution)/shard_map/ppermute | solution.py:494
  36.2 6.3 %collective-permute-start.16 = (bf16[4,32,2048]{2,1,0:T(8,128)(2,1)S(1)}, bf16[4,32,2048]{2,1,0:T(8,128)(2,1)S(1)}, u32[]{:S(2)}, u32[]{:S(2)}) collective-permute-start(bf16[4,32,2048]{2,1,0:T(8,128)(2,1)S(1)} %pad_maximum_fusion.refs_19_), channel_id=1, source_target_pairs={{0,1},{1,0},{2,3},{3,2},{4,5},{5,4},{6,7},{7,6},{8,9},{9,8},{10,11... | collective-permute-start | bytes 1572872 | tf_op jit(solution)/shard_map/ppermute | solution.py:494
  60.4 2.9 %collective-permute-start.17 = (bf16[256,2048]{1,0:T(8,128)(2,1)}, bf16[256,2048]{1,0:T(8,128)(2,1)S(1)}, u32[]{:S(2)}, u32[]{:S(2)}) collective-permute-start(bf16[256,2048]{1,0:T(8,128)(2,1)} %get-tuple-element.91), channel_id=1, source_target_pairs={{0,1},{1,0},{2,3},{3,2},{4,5},{5,4},{6,7},{7,6},{8,9},{9,8},{10,11... | collective-permute-start | bytes 3145736 | tf_op jit(solution)/shard_map/ppermute | solution.py:494
  64.9 6.3 %collective-permute-start.21 = (bf16[64,1024]{1,0:T(8,128)(2,1)S(1)}, bf16[64,1024]{1,0:T(8,128)(2,1)S(1)}, u32[]{:S(2)}, u32[]{:S(2)}) collective-permute-start(bf16[64,1024]{1,0:T(8,128)(2,1)S(1)} %get-tuple-element.99), channel_id=1, source_target_pairs={{0,2},{1,3},{2,0},{3,1},{4,6},{5,7},{6,4},{7,5},{8,10},{9,11},{10,... | collective-permute-start | bytes 393224 | tf_op jit(solution)/shard_map/ppermute | solution.py:498
  64.9 8.8 %collective-permute-start.18 = (bf16[64,1024]{1,0:T(8,128)(2,1)S(1)}, bf16[64,1024]{1,0:T(8,128)(2,1)S(1)}, u32[]{:S(2)}, u32[]{:S(2)}) collective-permute-start(bf16[64,1024]{1,0:T(8,128)(2,1)S(1)} %get-tuple-element.94), channel_id=1, source_target_pairs={{0,2},{1,3},{2,0},{3,1},{4,6},{5,7},{6,4},{7,5},{8,10},{9,11},{10,... | collective-permute-start | bytes 393224 | tf_op jit(solution)/shard_map/ppermute | solution.py:498
  71.3 10.3 %collective-permute-start.22 = (bf16[64,1024]{1,0:T(8,128)(2,1)S(1)}, bf16[64,1024]{1,0:T(8,128)(2,1)S(1)}, u32[]{:S(2)}, u32[]{:S(2)}) collective-permute-start(bf16[64,1024]{1,0:T(8,128)(2,1)S(1)} %add_convert_fusion.2), channel_id=1, source_target_pairs={{0,4},{1,5},{2,6},{3,7},{4,0},{5,1},{6,2},{7,3},{8,12},{9,13},{10,... | collective-permute-start | bytes 393224 | tf_op jit(solution)/shard_map/ppermute | solution.py:498
  71.7 7.7 %collective-permute-start.23 = (bf16[64,1024]{1,0:T(8,128)(2,1)S(1)}, bf16[64,1024]{1,0:T(8,128)(2,1)S(1)}, u32[]{:S(2)}, u32[]{:S(2)}) collective-permute-start(bf16[64,1024]{1,0:T(8,128)(2,1)S(1)} %get-tuple-element.101), channel_id=1, source_target_pairs={{0,2},{1,3},{2,0},{3,1},{4,6},{5,7},{6,4},{7,5},{8,10},{9,11},{10,... | collective-permute-start | bytes 393224 | tf_op jit(solution)/shard_map/ppermute | solution.py:498
  73.8 10.8 %collective-permute-start.19 = (bf16[64,1024]{1,0:T(8,128)(2,1)S(1)}, bf16[64,1024]{1,0:T(8,128)(2,1)S(1)}, u32[]{:S(2)}, u32[]{:S(2)}) collective-permute-start(bf16[64,1024]{1,0:T(8,128)(2,1)S(1)} %add_convert_fusion.3), channel_id=1, source_target_pairs={{0,4},{1,5},{2,6},{3,7},{4,0},{5,1},{6,2},{7,3},{8,12},{9,13},{10,... | collective-permute-start | bytes 393224 | tf_op jit(solution)/shard_map/ppermute | solution.py:498
  74.4 9.0 %collective-permute-start.20 = (bf16[64,1024]{1,0:T(8,128)(2,1)S(1)}, bf16[64,1024]{1,0:T(8,128)(2,1)S(1)}, u32[]{:S(2)}, u32[]{:S(2)}) collective-permute-start(bf16[64,1024]{1,0:T(8,128)(2,1)S(1)} %get-tuple-element.96), channel_id=1, source_target_pairs={{0,2},{1,3},{2,0},{3,1},{4,6},{5,7},{6,4},{7,5},{8,10},{9,11},{10,... | collective-permute-start | bytes 393224 | tf_op jit(solution)/shard_map/ppermute | solution.py:498
  87.5 13.3 %collective-permute-start.24 = (bf16[64,2048]{1,0:T(8,128)(2,1)}, bf16[64,2048]{1,0:T(8,128)(2,1)S(1)}, u32[]{:S(2)}, u32[]{:S(2)}) collective-permute-start(bf16[64,2048]{1,0:T(8,128)(2,1)} %get-tuple-element.113.refs_0_), channel_id=1, source_target_pairs={{0,2},{1,3},{2,0},{3,1},{4,6},{5,7},{6,4},{7,5},{8,10},{9,11},{10,... | collective-permute-start | bytes 786440 | tf_op jit(solution)/shard_map/ppermute | solution.py:498
  87.8 14.0 %collective-permute-start.25 = (bf16[64,2048]{1,0:T(8,128)(2,1)}, bf16[64,2048]{1,0:T(8,128)(2,1)S(1)}, u32[]{:S(2)}, u32[]{:S(2)}) collective-permute-start(bf16[64,2048]{1,0:T(8,128)(2,1)} %get-tuple-element.113.refs_0_), channel_id=1, source_target_pairs={{0,4},{1,5},{2,6},{3,7},{4,0},{5,1},{6,2},{7,3},{8,12},{9,13},{10,... | collective-permute-start | bytes 786440 | tf_op jit(solution)/shard_map/ppermute | solution.py:498
  101.7 6.4 %collective-permute-start.26 = (bf16[64,2048]{1,0:T(8,128)(2,1)S(1)}, bf16[64,2048]{1,0:T(8,128)(2,1)S(1)}, u32[]{:S(2)}, u32[]{:S(2)}) collective-permute-start(bf16[64,2048]{1,0:T(8,128)(2,1)S(1)} %collective-permute-done.25.refs_2_), channel_id=1, source_target_pairs={{0,2},{1,3},{2,0},{3,1},{4,6},{5,7},{6,4},{7,5},{8,10},{9,11},{10,... | collective-permute-start | bytes 786440 | tf_op jit(solution)/shard_map/ppermute | solution.py:498
  101.7 6.4 %collective-permute-start.29 = (bf16[64,2048]{1,0:T(8,128)(2,1)S(1)}, bf16[64,2048]{1,0:T(8,128)(2,1)S(1)}, u32[]{:S(2)}, u32[]{:S(2)}) collective-permute-start(bf16[64,2048]{1,0:T(8,128)(2,1)S(1)} %collective-permute-done.25.refs_2_), channel_id=1, source_target_pairs={{0,1},{1,0},{2,3},{3,2},{4,5},{5,4},{6,7},{7,6},{8,9},{9,8},{10,11... | collective-permute-start | bytes 786440 | tf_op jit(solution)/shard_map/ppermute | solution.py:494
  101.7 6.4 %collective-permute-start.27 = (bf16[64,2048]{1,0:T(8,128)(2,1)S(1)}, bf16[64,2048]{1,0:T(8,128)(2,1)S(1)}, u32[]{:S(2)}, u32[]{:S(2)}) collective-permute-start(bf16[64,2048]{1,0:T(8,128)(2,1)S(1)} %copy-done.8), channel_id=1, source_target_pairs={{0,1},{1,0},{2,3},{3,2},{4,5},{5,4},{6,7},{7,6},{8,9},{9,8},{10,11... | collective-permute-start | bytes 786440 | tf_op jit(solution)/shard_map/ppermute | solution.py:494
  102.2 5.9 %collective-permute-start.28 = (bf16[64,2048]{1,0:T(8,128)(2,1)S(1)}, bf16[64,2048]{1,0:T(8,128)(2,1)S(1)}, u32[]{:S(2)}, u32[]{:S(2)}) collective-permute-start(bf16[64,2048]{1,0:T(8,128)(2,1)S(1)} %collective-permute-done.24.refs_1_), channel_id=1, source_target_pairs={{0,1},{1,0},{2,3},{3,2},{4,5},{5,4},{6,7},{7,6},{8,9},{9,8},{10,11... | collective-permute-start | bytes 786440 | tf_op jit(solution)/shard_map/ppermute | solution.py:494
  153.7 6.4 %collective-permute-start.35 = (bf16[64,1024]{1,0:T(8,128)(2,1)S(1)}, bf16[64,1024]{1,0:T(8,128)(2,1)S(1)}, u32[]{:S(2)}, u32[]{:S(2)}) collective-permute-start(bf16[64,1024]{1,0:T(8,128)(2,1)S(1)} %get-tuple-element.125), channel_id=1, source_target_pairs={{0,2},{1,3},{2,0},{3,1},{4,6},{5,7},{6,4},{7,5},{8,10},{9,11},{10,... | collective-permute-start | bytes 393224 | tf_op jit(solution)/shard_map/ppermute | solution.py:498
  153.7 8.8 %collective-permute-start.32 = (bf16[64,1024]{1,0:T(8,128)(2,1)S(1)}, bf16[64,1024]{1,0:T(8,128)(2,1)S(1)}, u32[]{:S(2)}, u32[]{:S(2)}) collective-permute-start(bf16[64,1024]{1,0:T(8,128)(2,1)S(1)} %get-tuple-element.120), channel_id=1, source_target_pairs={{0,2},{1,3},{2,0},{3,1},{4,6},{5,7},{6,4},{7,5},{8,10},{9,11},{10,... | collective-permute-start | bytes 393224 | tf_op jit(solution)/shard_map/ppermute | solution.py:498
  160.1 11.5 %collective-permute-start.36 = (bf16[64,1024]{1,0:T(8,128)(2,1)S(1)}, bf16[64,1024]{1,0:T(8,128)(2,1)S(1)}, u32[]{:S(2)}, u32[]{:S(2)}) collective-permute-start(bf16[64,1024]{1,0:T(8,128)(2,1)S(1)} %add_convert_fusion), channel_id=1, source_target_pairs={{0,4},{1,5},{2,6},{3,7},{4,0},{5,1},{6,2},{7,3},{8,12},{9,13},{10,... | collective-permute-start | bytes 393224 | tf_op jit(solution)/shard_map/ppermute | solution.py:498
  160.6 11.0 %collective-permute-start.37 = (bf16[64,1024]{1,0:T(8,128)(2,1)S(1)}, bf16[64,1024]{1,0:T(8,128)(2,1)S(1)}, u32[]{:S(2)}, u32[]{:S(2)}) collective-permute-start(bf16[64,1024]{1,0:T(8,128)(2,1)S(1)} %get-tuple-element.127), channel_id=1, source_target_pairs={{0,2},{1,3},{2,0},{3,1},{4,6},{5,7},{6,4},{7,5},{8,10},{9,11},{10,... | collective-permute-start | bytes 393224 | tf_op jit(solution)/shard_map/ppermute | solution.py:498
  162.6 10.8 %collective-permute-start.34 = (bf16[64,1024]{1,0:T(8,128)(2,1)S(1)}, bf16[64,1024]{1,0:T(8,128)(2,1)S(1)}, u32[]{:S(2)}, u32[]{:S(2)}) collective-permute-start(bf16[64,1024]{1,0:T(8,128)(2,1)S(1)} %get-tuple-element.122), channel_id=1, source_target_pairs={{0,2},{1,3},{2,0},{3,1},{4,6},{5,7},{6,4},{7,5},{8,10},{9,11},{10,... | collective-permute-start | bytes 393224 | tf_op jit(solution)/shard_map/ppermute | solution.py:498
  162.8 10.7 %collective-permute-start.33 = (bf16[64,1024]{1,0:T(8,128)(2,1)S(1)}, bf16[64,1024]{1,0:T(8,128)(2,1)S(1)}, u32[]{:S(2)}, u32[]{:S(2)}) collective-permute-start(bf16[64,1024]{1,0:T(8,128)(2,1)S(1)} %add_convert_fusion.1), channel_id=1, source_target_pairs={{0,4},{1,5},{2,6},{3,7},{4,0},{5,1},{6,2},{7,3},{8,12},{9,13},{10,... | collective-permute-start | bytes 393224 | tf_op jit(solution)/shard_map/ppermute | solution.py:498
  (48 other events, 298.6 us)
where the time goes:
time: 177 us; the launch traced here: 176 us
  Pallas kernels  71.6 us (40%)
  waiting for transfers between devices  46.7 us (26%)
  starting transfers between devices  34.2 us (19%)
  local copies, waits for them, and re-layouts  11.7 us (7%)
  other arithmetic  10.2 us (6%)
    pallas_call x1, Pallas kernels, expert_layer(): pl.pallas_call(functools.partial(experts_kernel, len(pieces), capacity),...  40.1 us
    ppermute x21, waiting for transfers between devices, swap_chips(): lax.ppermute(value, 'tensor', [(i, i ^ 2 * by) for i in range(parts)])  38.7 us
    ppermute x21, starting transfers between devices, swap_chips(): lax.ppermute(value, 'tensor', [(i, i ^ 2 * by) for i in range(parts)])  26.1 us
    pallas_call x1, Pallas kernels, attention(): pl.pallas_call(functools.partial(attention_kernel, len(tokens), len(piece...  16.3 us
    pallas_call x1, Pallas kernels, fill_pages(): pl.pallas_call(pages_kernel, out_shape=jax.ShapeDtypeStruct((count, colum...  8.07 us
    ppermute x14, waiting for transfers between devices, other_core(): return lax.ppermute(value, 'tensor', [(i, i ^ 1) for i in range(parts)])  6.84 us
    unnamed x84, local copies, waits for them, and re-layouts  5.05 us
    ppermute x3, starting transfers between devices, swap_holder(): return lax.ppermute(value, 'dp', [(i, i ^ by) for i in range(holders)])  5 us
  transfers between devices with their start and end apart: 38, of which 20 were waited for; matrix products, arithmetic and copies ran while one was open for 9% of the time, Pallas kernels for 6%

commit v1 on v0

--- a/solution.py
+++ b/solution.py
@@ -136,8 +136,6 @@
     spot_ref,
     gain_ref,
     row_ref,
-    colslot_ref,
-    oslot_ref,
     cos_ref,
     sin_ref,
     qg_ref,
@@ -192,7 +190,15 @@
     ]
     for copy in last_copies:
         copy.start()
-    factors = s_ref.shape[0] * s_ref.shape[1]
+    adapters, ranks = s_ref.shape[:2]
+    factors = adapters * ranks
+
+    def own_slot(low, slot):
+        count = low.shape[1] // adapters
+        column = lax.broadcasted_iota(jnp.int32, (1, low.shape[1]), 1).astype(F32)
+        keep = (column >= slot * count) & (column < slot * count + count)
+        return jnp.where(keep, low, 0.0).astype(BF16)
+
     gain = gain_ref[...].astype(F32)
     qg = qg_ref[...].astype(F32)
     kg = kg_ref[...].astype(F32)
@@ -220,7 +226,7 @@
     def adapt(i, carry):
         here = pl.ds(pl.multiple_of(i * block, block), block)
         low = dot_nt(x_ref[here, :], s_ref[...].reshape(factors, width))
-        low = jnp.where(meta_ref[here, 0:1] == colslot_ref[...], low, 0.0).astype(BF16)
+        low = own_slot(low, meta_ref[here, 0:1])
         delta = ADAPTER_FACTOR * dot(low, up_ref[...])
         q = qf_ref[here, :] + delta[:, :query_cols]
         kv = (kvf_ref[here, :] + delta[:, query_cols:]).astype(BF16)
@@ -253,7 +259,7 @@
                 heads_mixed.append(mixed.astype(BF16))
             mixed = jnp.concatenate(heads_mixed, axis=1)
             low = dot_nt(mixed, sho_ref[...])
-            low = jnp.where(meta_ref[here, 0:1] == oslot_ref[...], low, 0.0).astype(BF16)
+            low = own_slot(low, meta_ref[here, 0:1])
             step = min(512, width)
             for c in range(0, width, step):
                 cut = slice(c, c + step)
@@ -280,7 +286,7 @@
     return pl.pallas_call(
         functools.partial(attention_kernel, len(tokens), len(pieces), len(parts)),
         out_shape=(half, half, jax.ShapeDtypeStruct((rows, 2 * head), BF16)),
-        in_specs=[SMEM] + [VMEM] * 9 + [ANY] * (4 + len(tokens) + len(pieces) + len(parts)),
+        in_specs=[SMEM] + [VMEM] * 7 + [ANY] * (4 + len(tokens) + len(pieces) + len(parts)),
         out_specs=(VMEM, VMEM, VMEM),
         scratch_shapes=[
             pltpu.VMEM(wq.shape, BF16),
@@ -625,8 +631,6 @@
     cosine, sine = jnp.cos(angle), jnp.sin(angle)
     cosine = jnp.concatenate([cosine, cosine], axis=1)
     sine = jnp.concatenate([-sine, sine], axis=1)
-    colslot = (jnp.arange(adapters * ranks, dtype=jnp.int32) // ranks)[None, :].astype(F32)
-    oslot = (jnp.arange(adapters * rank, dtype=jnp.int32) // rank)[None, :].astype(F32)
 
     up_kv = lax.dynamic_index_in_dim(
         key_value_up_factors.reshape(adapters, rank, kv_heads, 2, head_length), head, 2, keepdims=False
@@ -650,10 +654,13 @@
         w_o,
         expand_o.reshape(adapters * rank, width),
     )
-    meta = (meta_row, colslot, oslot, cosine, sine)
+    meta = (meta_row, cosine, sine)
     half = held // 2
     half_own = lax.dynamic_slice_in_dim(shrink_qkv, core * half, half, 0)
-    halves = [swap_holder(half_own, holders, r) for r in range(1, holders)]
+    halves = []
+    for r in range(1, holders):
+        top = 1 << (r.bit_length() - 1)
+        halves.append(swap_holder(half_own if r == top else halves[r - top - 1], holders, top))
     spots = [chip, core, holder * held]
     for r in range(1, holders):
         begin = (holder ^ r) * held

time: 177 us -> 176 us (level)
  waiting for transfers between devices: 46.7 us -> 51 us
  starting transfers between devices: 34.2 us -> 30.6 us
    ppermute x21, waiting for transfers between devices: 38.7 us -> 44.3 us  [swap_chips(): lax.ppermute(value, 'tensor', [(i, i ^ 2 * by) for i in range(parts)])]
    ppermute x21, starting transfers between devices: 26.1 us -> 22.6 us  [swap_chips(): lax.ppermute(value, 'tensor', [(i, i ^ 2 * by) for i in range(parts)])]
  transfers between devices with their start and end apart: 38 -> 38, of which waited for: 20 -> 22; matrix products, arithmetic and copies ran while one was open for 9% -> 9% of each run, Pallas kernels for 6% -> 6%
where the time goes in v1:
time: 176 us
  Pallas kernels  71.6 us (41%)
  waiting for transfers between devices  51 us (29%)
  starting transfers between devices  30.6 us (17%)
  local copies, waits for them, and re-layouts  12 us (7%)
  other arithmetic  9.08 us (5%)
    ppermute x21, waiting for transfers between devices, swap_chips(): lax.ppermute(value, 'tensor', [(i, i ^ 2 * by) for i in range(parts)])  44.3 us
    pallas_call x1, Pallas kernels, expert_layer(): pl.pallas_call(functools.partial(experts_kernel, len(pieces), capacity),...  40.1 us
    ppermute x21, starting transfers between devices, swap_chips(): lax.ppermute(value, 'tensor', [(i, i ^ 2 * by) for i in range(parts)])  22.6 us
    pallas_call x1, Pallas kernels, attention(): pl.pallas_call(functools.partial(attention_kernel, len(tokens), len(piece...  16.3 us
    pallas_call x1, Pallas kernels, fill_pages(): pl.pallas_call(pages_kernel, out_shape=jax.ShapeDtypeStruct((count, colum...  8.07 us
    ppermute x14, waiting for transfers between devices, other_core(): return lax.ppermute(value, 'tensor', [(i, i ^ 1) for i in range(parts)])  6.69 us
    unnamed x84, local copies, waits for them, and re-layouts  5.24 us
    ppermute x3, starting transfers between devices, swap_holder(): return lax.ppermute(value, 'dp', [(i, i ^ by) for i in range(holders)])  5.03 us
  transfers between devices with their start and end apart: 38, of which 22 were waited for; matrix products, arithmetic and copies ran while one was open for 9% of the time, Pallas kernels for 6%

profile of v1, /device:TPU:0, one launch (start us, length us, event | category | flops | bytes accessed | tf_op | source)
XLA Modules:
  0.0 175.9 jit_solution(10726789719552141560)
XLA Ops:
  1.8 3.0 %collective-permute-start.2 = (bf16[2,48,2048]{2,1,0:T(8,128)(2,1)S(1)}, bf16[2,48,2048]{2,1,0:T(8,128)(2,1)S(1)}, u32[]{:S(2)}, u32[]{:S(2)}) collective-permute-start(bf16[2,48,2048]{2,1,0:T(8,128)(2,1)S(1)} %constant_dynamic-slice_fusion.6), channel_id=1, source_target_pairs={{0,8},{8,0},{16,24},{24,16},{1,9},{9,1},{17,25},{25,17},{2,10},{10... | collective-permute-start | bytes 1179656 | tf_op jit(solution)/shard_map/ppermute | solution.py:508
  4.8 1.5 collective-permute-start.3
  6.3 1.6 collective-permute-start
  7.9 2.6 %collective-permute-start.1 = (bf16[64,2048]{1,0:T(8,128)(2,1)}, bf16[64,2048]{1,0:T(8,128)(2,1)}, u32[]{:S(2)}, u32[]{:S(2)}) collective-permute-start(bf16[64,2048]{1,0:T(8,128)(2,1)} %x_ref.1), channel_id=1, source_target_pairs={{0,4},{1,5},{2,6},{3,7},{4,0},{5,1},{6,2},{7,3},{8,12},{9,13},{10,... | collective-permute-start | bytes 786440 | tf_op jit(solution)/shard_map/ppermute | solution.py:504
  20.0 2.1 %collective-permute-done.1.refs_6_ = bf16[64,2048]{1,0:T(8,128)(2,1)} collective-permute-done((bf16[64,2048]{1,0:T(8,128)(2,1)}, bf16[64,2048]{1,0:T(8,128)(2,1)}, u32[]{:S(2)}, u32[]{:S(2)}) %collective-permute-start.1) | collective-permute-done | bytes 262176 | tf_op jit(solution)/shard_map/ppermute | solution.py:504
  22.5 2.7 %collective-permute-start.5 = (bf16[32,2048]{1,0:T(8,128)(2,1)S(1)}, bf16[32,2048]{1,0:T(8,128)(2,1)S(1)}, u32[]{:S(2)}, u32[]{:S(2)}) collective-permute-start(bf16[32,2048]{1,0:T(8,128)(2,1)S(1)} %get-tuple-element.66), channel_id=1, source_target_pairs={{0,4},{1,5},{2,6},{3,7},{4,0},{5,1},{6,2},{7,3},{8,12},{9,13},{10,... | collective-permute-start | bytes 393224 | tf_op jit(solution)/shard_map/ppermute | solution.py:504
  29.4 3.9 %collective-permute-done.4 = bf16[32,2048]{1,0:T(8,128)(2,1)S(1)} collective-permute-done((bf16[32,2048]{1,0:T(8,128)(2,1)S(1)}, bf16[32,2048]{1,0:T(8,128)(2,1)S(1)}, u32[]{:S(2)}, u32[]{:S(2)}) %collective-permute-start.4) | collective-permute-done | bytes 131104 | tf_op jit(solution)/shard_map/ppermute | solution.py:504
  34.2 3.8 %collective-permute-done.7.refs_7_ = bf16[64,2048]{1,0:T(8,128)(2,1)} collective-permute-done((bf16[64,2048]{1,0:T(8,128)(2,1)}, bf16[64,2048]{1,0:T(8,128)(2,1)}, u32[]{:S(2)}, u32[]{:S(2)}) %collective-permute-start.7) | collective-permute-done | bytes 262176 | tf_op jit(solution)/shard_map/ppermute | solution.py:504
  43.7 16.3 %attention.1 = (bf16[256,2048]{1,0:T(8,128)(2,1)}, bf16[256,2048]{1,0:T(8,128)(2,1)}, bf16[512,256]{1,0:T(8,128)(2,1)}) custom-call(s32[9]{0:T(128)} %stack.77.spot_ref, bf16[1,2048]{1,0:T(2,128)(2,1)} %reshape.313.gain_ref, f32[8,512]{1,0:T(8,128)} %convert_element_type.68.row_ref, f32[512,128]{1,0:T(8,128)} %pad_maximum_fusion.1.cos_ref, ...), custom_call_target="tpu_custom_call" | custom-call | flops 4563402752 | bytes 16777216 | tf_op jit(solution)/shard_map/attention/pallas_call | solution.py:286
  61.5 1.5 collective-permute-done.17.b_ref
  64.5 2.1 %collective-permute-start.18 = (bf16[64,1024]{1,0:T(8,128)(2,1)S(1)}, bf16[64,1024]{1,0:T(8,128)(2,1)S(1)}, u32[]{:S(2)}, u32[]{:S(2)}) collective-permute-start(bf16[64,1024]{1,0:T(8,128)(2,1)S(1)} %get-tuple-element.90), channel_id=1, source_target_pairs={{0,2},{1,3},{2,0},{3,1},{4,6},{5,7},{6,4},{7,5},{8,10},{9,11},{10,... | collective-permute-start | bytes 393224 | tf_op jit(solution)/shard_map/ppermute | solution.py:504
  66.6 4.2 %collective-permute-done.21 = bf16[64,1024]{1,0:T(8,128)(2,1)S(1)} collective-permute-done((bf16[64,1024]{1,0:T(8,128)(2,1)S(1)}, bf16[64,1024]{1,0:T(8,128)(2,1)S(1)}, u32[]{:S(2)}, u32[]{:S(2)}) %collective-permute-start.21) | collective-permute-done | bytes 131104 | tf_op jit(solution)/shard_map/ppermute | solution.py:504
  70.9 1.4 collective-permute-start.23
  74.0 2.0 %collective-permute-start.20 = (bf16[64,1024]{1,0:T(8,128)(2,1)S(1)}, bf16[64,1024]{1,0:T(8,128)(2,1)S(1)}, u32[]{:S(2)}, u32[]{:S(2)}) collective-permute-start(bf16[64,1024]{1,0:T(8,128)(2,1)S(1)} %get-tuple-element.92), channel_id=1, source_target_pairs={{0,2},{1,3},{2,0},{3,1},{4,6},{5,7},{6,4},{7,5},{8,10},{9,11},{10,... | collective-permute-start | bytes 393224 | tf_op jit(solution)/shard_map/ppermute | solution.py:504
  76.6 2.9 %collective-permute-done.23.refs_5_ = bf16[64,1024]{1,0:T(8,128)(2,1)S(1)} collective-permute-done((bf16[64,1024]{1,0:T(8,128)(2,1)S(1)}, bf16[64,1024]{1,0:T(8,128)(2,1)S(1)}, u32[]{:S(2)}, u32[]{:S(2)}) %collective-permute-start.23) | collective-permute-done | bytes 131104 | tf_op jit(solution)/shard_map/ppermute | solution.py:504
  79.5 1.6 collective-permute-done.22.refs_4_
  81.1 1.8 %collective-permute-done.20.refs_2_ = bf16[64,1024]{1,0:T(8,128)(2,1)S(1)} collective-permute-done((bf16[64,1024]{1,0:T(8,128)(2,1)S(1)}, bf16[64,1024]{1,0:T(8,128)(2,1)S(1)}, u32[]{:S(2)}, u32[]{:S(2)}) %collective-permute-start.20) | collective-permute-done | bytes 131104 | tf_op jit(solution)/shard_map/ppermute | solution.py:504
  84.8 2.2 %residual_norm.1 = (bf16[64,2048]{1,0:T(8,128)(2,1)}, bf16[64,2048]{1,0:T(8,128)(2,1)}) custom-call(bf16[64,2048]{1,0:T(8,128)(2,1)} %x_ref.1, bf16[1,2048]{1,0:T(2,128)(2,1)} %reshape.310.gain_ref, bf16[64,1024]{1,0:T(8,128)(2,1)} %copy-done, bf16[64,1024]{1,0:T(8,128)(2,1)} %copy-done.20, bf16[64,1024]{1,0:T(8,128)(2,1)} %copy-done.21, ...), custom_call_target="tpu_custom_call" | custom-call | tf_op jit(solution)/shard_map/residual_norm/pallas_call | solution.py:66
  87.3 1.5 collective-permute-start.25
  91.5 8.1 %fill_pages.1 = bf16[64,128,128]{2,1,0:T(8,128)(2,1)} custom-call(s32[64]{0:T(128)S(1)} %add.258.first_ref, s32[64]{0:T(128)S(1)} %min.12.length_ref, s32[64]{0:T(128)S(1)} %bitcast.85, bf16[128,640]{1,0:T(8,128)(2,1)S(1)} %pad.19.entries_ref), custom_call_target="tpu_custom_call" | custom-call | flops 2147483648 | bytes 4194304 | tf_op jit(solution)/shard_map/fill_pages/pallas_call | solution.py:349
  99.6 1.7 collective-permute-done.25.refs_2_
  101.9 6.1 %collective-permute-done.26.refs_3_ = bf16[64,2048]{1,0:T(8,128)(2,1)S(1)} collective-permute-done((bf16[64,2048]{1,0:T(8,128)(2,1)S(1)}, bf16[64,2048]{1,0:T(8,128)(2,1)S(1)}, u32[]{:S(2)}, u32[]{:S(2)}) %collective-permute-start.26) | collective-permute-done | bytes 262176 | tf_op jit(solution)/shard_map/ppermute | solution.py:504
  108.1 1.5 collective-permute-done.30.refs_7_
  110.3 40.1 %experts.1 = (bf16[256,2048]{1,0:T(8,128)(2,1)}, bf16[256,2048]{1,0:T(8,128)(2,1)}) custom-call(f32[16,512]{1,0:T(8,128)} %pad_maximum_fusion.3.route_ref, bf16[64,2048]{1,0:T(8,128)(2,1)} %get-tuple-element.109.refs_0_, bf16[64,2048]{1,0:T(8,128)(2,1)} %copy-done.9, bf16[64,2048]{1,0:T(8,128)(2,1)} %copy-done.10, bf16[64,2048]{1,0:T(8,128)(2,1)} %copy-done.11, ...), custom_call_target="tpu_custom_call" | custom-call | flops 9663676416 | bytes 75497472 | tf_op jit(solution)/shard_map/experts/pallas_call | solution.py:473
  151.8 1.5 collective-permute-done.31.b_ref
  153.9 1.7 collective-permute-start.32
  155.7 4.3 %collective-permute-done.35 = bf16[64,1024]{1,0:T(8,128)(2,1)S(1)} collective-permute-done((bf16[64,1024]{1,0:T(8,128)(2,1)S(1)}, bf16[64,1024]{1,0:T(8,128)(2,1)S(1)}, u32[]{:S(2)}, u32[]{:S(2)}) %collective-permute-start.35) | collective-permute-done | bytes 131104 | tf_op jit(solution)/shard_map/ppermute | solution.py:504
  160.2 1.6 collective-permute-start.37
  163.1 2.0 %collective-permute-start.33 = (bf16[64,1024]{1,0:T(8,128)(2,1)S(1)}, bf16[64,1024]{1,0:T(8,128)(2,1)S(1)}, u32[]{:S(2)}, u32[]{:S(2)}) collective-permute-start(bf16[64,1024]{1,0:T(8,128)(2,1)S(1)} %add_convert_fusion.1), channel_id=1, source_target_pairs={{0,4},{1,5},{2,6},{3,7},{4,0},{5,1},{6,2},{7,3},{8,12},{9,13},{10,... | collective-permute-start | bytes 393224 | tf_op jit(solution)/shard_map/ppermute | solution.py:504
  165.2 6.6 %collective-permute-done.37.refs_5_ = bf16[64,1024]{1,0:T(8,128)(2,1)S(1)} collective-permute-done((bf16[64,1024]{1,0:T(8,128)(2,1)S(1)}, bf16[64,1024]{1,0:T(8,128)(2,1)S(1)}, u32[]{:S(2)}, u32[]{:S(2)}) %collective-permute-start.37) | collective-permute-done | bytes 131104 | tf_op jit(solution)/shard_map/ppermute | solution.py:504
  171.8 1.4 collective-permute-done.34.refs_2_
  173.9 2.0 %total_rows.1 = bf16[64,2048]{1,0:T(8,128)(2,1)} custom-call(bf16[64,1024]{1,0:T(8,128)(2,1)} %copy-done.2, bf16[64,1024]{1,0:T(8,128)(2,1)} %copy-done.25, bf16[64,1024]{1,0:T(8,128)(2,1)} %copy-done.24, bf16[64,1024]{1,0:T(8,128)(2,1)} %copy-done.3, bf16[64,1024]{1,0:T(8,128)(2,1)} %copy-done.22, bf16[64,1024]{1,0:T(8,128)(2,1)} %copy-done.23), custom_call_target="tpu_custom_call" | custom-call | tf_op jit(solution)/shard_map/total_rows/pallas_call | solution.py:84
  (208 shorter events, 37.2 us)
Async XLA Ops:
  1.8 20.3 %collective-permute-start.2 = (bf16[2,48,2048]{2,1,0:T(8,128)(2,1)S(1)}, bf16[2,48,2048]{2,1,0:T(8,128)(2,1)S(1)}, u32[]{:S(2)}, u32[]{:S(2)}) collective-permute-start(bf16[2,48,2048]{2,1,0:T(8,128)(2,1)S(1)} %constant_dynamic-slice_fusion.6), channel_id=1, source_target_pairs={{0,8},{8,0},{16,24},{24,16},{1,9},{9,1},{17,25},{25,17},{2,10},{10... | collective-permute-start | bytes 1179656 | tf_op jit(solution)/shard_map/ppermute | solution.py:508
  4.8 17.3 %collective-permute-start.3 = (bf16[2,48,2048]{2,1,0:T(8,128)(2,1)S(1)}, bf16[2,48,2048]{2,1,0:T(8,128)(2,1)}, u32[]{:S(2)}, u32[]{:S(2)}) collective-permute-start(bf16[2,48,2048]{2,1,0:T(8,128)(2,1)S(1)} %constant_dynamic-slice_fusion.6), channel_id=1, source_target_pairs={{0,16},{8,24},{16,0},{24,8},{1,17},{9,25},{17,1},{25,9},{2,18},{10... | collective-permute-start | bytes 1179656 | tf_op jit(solution)/shard_map/ppermute | solution.py:508
  6.3 13.7 %collective-permute-start = (bf16[64,2048]{1,0:T(8,128)(2,1)}, bf16[64,2048]{1,0:T(8,128)(2,1)S(1)}, u32[]{:S(2)}, u32[]{:S(2)}) collective-permute-start(bf16[64,2048]{1,0:T(8,128)(2,1)} %x_ref.1), channel_id=1, source_target_pairs={{0,2},{1,3},{2,0},{3,1},{4,6},{5,7},{6,4},{7,5},{8,10},{9,11},{10,... | collective-permute-start | bytes 786440 | tf_op jit(solution)/shard_map/ppermute | solution.py:504
  7.9 14.2 %collective-permute-start.1 = (bf16[64,2048]{1,0:T(8,128)(2,1)}, bf16[64,2048]{1,0:T(8,128)(2,1)}, u32[]{:S(2)}, u32[]{:S(2)}) collective-permute-start(bf16[64,2048]{1,0:T(8,128)(2,1)} %x_ref.1), channel_id=1, source_target_pairs={{0,4},{1,5},{2,6},{3,7},{4,0},{5,1},{6,2},{7,3},{8,12},{9,13},{10,... | collective-permute-start | bytes 786440 | tf_op jit(solution)/shard_map/ppermute | solution.py:504
  22.1 11.1 %collective-permute-start.4 = (bf16[32,2048]{1,0:T(8,128)(2,1)S(1)}, bf16[32,2048]{1,0:T(8,128)(2,1)S(1)}, u32[]{:S(2)}, u32[]{:S(2)}) collective-permute-start(bf16[32,2048]{1,0:T(8,128)(2,1)S(1)} %get-tuple-element.65), channel_id=1, source_target_pairs={{0,2},{1,3},{2,0},{3,1},{4,6},{5,7},{6,4},{7,5},{8,10},{9,11},{10,... | collective-permute-start | bytes 393224 | tf_op jit(solution)/shard_map/ppermute | solution.py:504
  22.5 10.7 %collective-permute-start.5 = (bf16[32,2048]{1,0:T(8,128)(2,1)S(1)}, bf16[32,2048]{1,0:T(8,128)(2,1)S(1)}, u32[]{:S(2)}, u32[]{:S(2)}) collective-permute-start(bf16[32,2048]{1,0:T(8,128)(2,1)S(1)} %get-tuple-element.66), channel_id=1, source_target_pairs={{0,4},{1,5},{2,6},{3,7},{4,0},{5,1},{6,2},{7,3},{8,12},{9,13},{10,... | collective-permute-start | bytes 393224 | tf_op jit(solution)/shard_map/ppermute | solution.py:504
  25.2 9.0 %collective-permute-start.6 = (bf16[32,2048]{1,0:T(8,128)(2,1)S(1)}, bf16[32,2048]{1,0:T(8,128)(2,1)S(1)}, u32[]{:S(2)}, u32[]{:S(2)}) collective-permute-start(bf16[32,2048]{1,0:T(8,128)(2,1)S(1)} %get-tuple-element.67), channel_id=1, source_target_pairs={{0,6},{1,7},{2,4},{3,5},{4,2},{5,3},{6,0},{7,1},{8,14},{9,15},{10,... | collective-permute-start | bytes 393224 | tf_op jit(solution)/shard_map/ppermute | solution.py:504
  26.6 11.5 %collective-permute-start.7 = (bf16[64,2048]{1,0:T(8,128)(2,1)}, bf16[64,2048]{1,0:T(8,128)(2,1)}, u32[]{:S(2)}, u32[]{:S(2)}) collective-permute-start(bf16[64,2048]{1,0:T(8,128)(2,1)} %collective-permute-done.1.refs_6_), channel_id=1, source_target_pairs={{0,2},{1,3},{2,0},{3,1},{4,6},{5,7},{6,4},{7,5},{8,10},{9,11},{10,... | collective-permute-start | bytes 786440 | tf_op jit(solution)/shard_map/ppermute | solution.py:504
  26.6 12.7 %collective-permute-start.14 = (bf16[2,48,2048]{2,1,0:T(8,128)(2,1)S(1)}, bf16[2,48,2048]{2,1,0:T(8,128)(2,1)S(1)}, u32[]{:S(2)}, u32[]{:S(2)}) collective-permute-start(bf16[2,48,2048]{2,1,0:T(8,128)(2,1)S(1)} %collective-permute-done.2.refs_13_), channel_id=1, source_target_pairs={{0,16},{8,24},{16,0},{24,8},{1,17},{9,25},{17,1},{25,9},{2,18},{10... | collective-permute-start | bytes 1179656 | tf_op jit(solution)/shard_map/ppermute | solution.py:508
  33.2 4.8 %collective-permute-start.10 = (bf16[64,2048]{1,0:T(8,128)(2,1)}, bf16[64,2048]{1,0:T(8,128)(2,1)S(1)}, u32[]{:S(2)}, u32[]{:S(2)}) collective-permute-start(bf16[64,2048]{1,0:T(8,128)(2,1)} %collective-permute-done.1.refs_6_), channel_id=1, source_target_pairs={{0,1},{1,0},{2,3},{3,2},{4,5},{5,4},{6,7},{7,6},{8,9},{9,8},{10,11... | collective-permute-start | bytes 786440 | tf_op jit(solution)/shard_map/ppermute | solution.py:500
  33.2 5.5 %collective-permute-start.8 = (bf16[64,2048]{1,0:T(8,128)(2,1)S(1)}, bf16[64,2048]{1,0:T(8,128)(2,1)}, u32[]{:S(2)}, u32[]{:S(2)}) collective-permute-start(bf16[64,2048]{1,0:T(8,128)(2,1)S(1)} %copy-done.17), channel_id=1, source_target_pairs={{0,1},{1,0},{2,3},{3,2},{4,5},{5,4},{6,7},{7,6},{8,9},{9,8},{10,11... | collective-permute-start | bytes 786440 | tf_op jit(solution)/shard_map/ppermute | solution.py:500
  34.1 5.2 %collective-permute-start.9 = (bf16[64,2048]{1,0:T(8,128)(2,1)S(1)}, bf16[64,2048]{1,0:T(8,128)(2,1)S(1)}, u32[]{:S(2)}, u32[]{:S(2)}) collective-permute-start(bf16[64,2048]{1,0:T(8,128)(2,1)S(1)} %collective-permute-done.refs_5_), channel_id=1, source_target_pairs={{0,1},{1,0},{2,3},{3,2},{4,5},{5,4},{6,7},{7,6},{8,9},{9,8},{10,11... | collective-permute-start | bytes 786440 | tf_op jit(solution)/shard_map/ppermute | solution.py:500
  38.0 4.0 %collective-permute-start.16 = (bf16[4,32,2048]{2,1,0:T(8,128)(2,1)S(1)}, bf16[4,32,2048]{2,1,0:T(8,128)(2,1)S(1)}, u32[]{:S(2)}, u32[]{:S(2)}) collective-permute-start(bf16[4,32,2048]{2,1,0:T(8,128)(2,1)S(1)} %pad_maximum_fusion.refs_19_), channel_id=1, source_target_pairs={{0,1},{1,0},{2,3},{3,2},{4,5},{5,4},{6,7},{7,6},{8,9},{9,8},{10,11... | collective-permute-start | bytes 1572872 | tf_op jit(solution)/shard_map/ppermute | solution.py:500
  38.0 3.0 %collective-permute-start.12 = (bf16[2,48,2048]{2,1,0:T(8,128)(2,1)S(1)}, bf16[2,48,2048]{2,1,0:T(8,128)(2,1)S(1)}, u32[]{:S(2)}, u32[]{:S(2)}) collective-permute-start(bf16[2,48,2048]{2,1,0:T(8,128)(2,1)S(1)} %collective-permute-done.2.refs_13_), channel_id=1, source_target_pairs={{0,1},{1,0},{2,3},{3,2},{4,5},{5,4},{6,7},{7,6},{8,9},{9,8},{10,11... | collective-permute-start | bytes 1179656 | tf_op jit(solution)/shard_map/ppermute | solution.py:500
  64.5 6.3 %collective-permute-start.21 = (bf16[64,1024]{1,0:T(8,128)(2,1)S(1)}, bf16[64,1024]{1,0:T(8,128)(2,1)S(1)}, u32[]{:S(2)}, u32[]{:S(2)}) collective-permute-start(bf16[64,1024]{1,0:T(8,128)(2,1)S(1)} %get-tuple-element.95), channel_id=1, source_target_pairs={{0,2},{1,3},{2,0},{3,1},{4,6},{5,7},{6,4},{7,5},{8,10},{9,11},{10,... | collective-permute-start | bytes 393224 | tf_op jit(solution)/shard_map/ppermute | solution.py:504
  64.5 9.1 %collective-permute-start.18 = (bf16[64,1024]{1,0:T(8,128)(2,1)S(1)}, bf16[64,1024]{1,0:T(8,128)(2,1)S(1)}, u32[]{:S(2)}, u32[]{:S(2)}) collective-permute-start(bf16[64,1024]{1,0:T(8,128)(2,1)S(1)} %get-tuple-element.90), channel_id=1, source_target_pairs={{0,2},{1,3},{2,0},{3,1},{4,6},{5,7},{6,4},{7,5},{8,10},{9,11},{10,... | collective-permute-start | bytes 393224 | tf_op jit(solution)/shard_map/ppermute | solution.py:504
  70.9 10.3 %collective-permute-start.22 = (bf16[64,1024]{1,0:T(8,128)(2,1)S(1)}, bf16[64,1024]{1,0:T(8,128)(2,1)S(1)}, u32[]{:S(2)}, u32[]{:S(2)}) collective-permute-start(bf16[64,1024]{1,0:T(8,128)(2,1)S(1)} %add_convert_fusion.2), channel_id=1, source_target_pairs={{0,4},{1,5},{2,6},{3,7},{4,0},{5,1},{6,2},{7,3},{8,12},{9,13},{10,... | collective-permute-start | bytes 393224 | tf_op jit(solution)/shard_map/ppermute | solution.py:504
  70.9 8.6 %collective-permute-start.23 = (bf16[64,1024]{1,0:T(8,128)(2,1)S(1)}, bf16[64,1024]{1,0:T(8,128)(2,1)S(1)}, u32[]{:S(2)}, u32[]{:S(2)}) collective-permute-start(bf16[64,1024]{1,0:T(8,128)(2,1)S(1)} %get-tuple-element.97), channel_id=1, source_target_pairs={{0,2},{1,3},{2,0},{3,1},{4,6},{5,7},{6,4},{7,5},{8,10},{9,11},{10,... | collective-permute-start | bytes 393224 | tf_op jit(solution)/shard_map/ppermute | solution.py:504
  73.7 10.5 %collective-permute-start.19 = (bf16[64,1024]{1,0:T(8,128)(2,1)S(1)}, bf16[64,1024]{1,0:T(8,128)(2,1)S(1)}, u32[]{:S(2)}, u32[]{:S(2)}) collective-permute-start(bf16[64,1024]{1,0:T(8,128)(2,1)S(1)} %add_convert_fusion.3), channel_id=1, source_target_pairs={{0,4},{1,5},{2,6},{3,7},{4,0},{5,1},{6,2},{7,3},{8,12},{9,13},{10,... | collective-permute-start | bytes 393224 | tf_op jit(solution)/shard_map/ppermute | solution.py:504
  74.0 9.0 %collective-permute-start.20 = (bf16[64,1024]{1,0:T(8,128)(2,1)S(1)}, bf16[64,1024]{1,0:T(8,128)(2,1)S(1)}, u32[]{:S(2)}, u32[]{:S(2)}) collective-permute-start(bf16[64,1024]{1,0:T(8,128)(2,1)S(1)} %get-tuple-element.92), channel_id=1, source_target_pairs={{0,2},{1,3},{2,0},{3,1},{4,6},{5,7},{6,4},{7,5},{8,10},{9,11},{10,... | collective-permute-start | bytes 393224 | tf_op jit(solution)/shard_map/ppermute | solution.py:504
  87.0 12.5 %collective-permute-start.24 = (bf16[64,2048]{1,0:T(8,128)(2,1)}, bf16[64,2048]{1,0:T(8,128)(2,1)S(1)}, u32[]{:S(2)}, u32[]{:S(2)}) collective-permute-start(bf16[64,2048]{1,0:T(8,128)(2,1)} %get-tuple-element.109.refs_0_), channel_id=1, source_target_pairs={{0,2},{1,3},{2,0},{3,1},{4,6},{5,7},{6,4},{7,5},{8,10},{9,11},{10,... | collective-permute-start | bytes 786440 | tf_op jit(solution)/shard_map/ppermute | solution.py:504
  87.3 14.0 %collective-permute-start.25 = (bf16[64,2048]{1,0:T(8,128)(2,1)}, bf16[64,2048]{1,0:T(8,128)(2,1)S(1)}, u32[]{:S(2)}, u32[]{:S(2)}) collective-permute-start(bf16[64,2048]{1,0:T(8,128)(2,1)} %get-tuple-element.109.refs_0_), channel_id=1, source_target_pairs={{0,4},{1,5},{2,6},{3,7},{4,0},{5,1},{6,2},{7,3},{8,12},{9,13},{10,... | collective-permute-start | bytes 786440 | tf_op jit(solution)/shard_map/ppermute | solution.py:504
  101.3 6.7 %collective-permute-start.26 = (bf16[64,2048]{1,0:T(8,128)(2,1)S(1)}, bf16[64,2048]{1,0:T(8,128)(2,1)S(1)}, u32[]{:S(2)}, u32[]{:S(2)}) collective-permute-start(bf16[64,2048]{1,0:T(8,128)(2,1)S(1)} %collective-permute-done.25.refs_2_), channel_id=1, source_target_pairs={{0,2},{1,3},{2,0},{3,1},{4,6},{5,7},{6,4},{7,5},{8,10},{9,11},{10,... | collective-permute-start | bytes 786440 | tf_op jit(solution)/shard_map/ppermute | solution.py:504
  101.3 6.8 %collective-permute-start.29 = (bf16[64,2048]{1,0:T(8,128)(2,1)S(1)}, bf16[64,2048]{1,0:T(8,128)(2,1)S(1)}, u32[]{:S(2)}, u32[]{:S(2)}) collective-permute-start(bf16[64,2048]{1,0:T(8,128)(2,1)S(1)} %collective-permute-done.25.refs_2_), channel_id=1, source_target_pairs={{0,1},{1,0},{2,3},{3,2},{4,5},{5,4},{6,7},{7,6},{8,9},{9,8},{10,11... | collective-permute-start | bytes 786440 | tf_op jit(solution)/shard_map/ppermute | solution.py:500
  101.3 6.7 %collective-permute-start.27 = (bf16[64,2048]{1,0:T(8,128)(2,1)S(1)}, bf16[64,2048]{1,0:T(8,128)(2,1)S(1)}, u32[]{:S(2)}, u32[]{:S(2)}) collective-permute-start(bf16[64,2048]{1,0:T(8,128)(2,1)S(1)} %copy-done.8), channel_id=1, source_target_pairs={{0,1},{1,0},{2,3},{3,2},{4,5},{5,4},{6,7},{7,6},{8,9},{9,8},{10,11... | collective-permute-start | bytes 786440 | tf_op jit(solution)/shard_map/ppermute | solution.py:500
  101.8 6.2 %collective-permute-start.28 = (bf16[64,2048]{1,0:T(8,128)(2,1)S(1)}, bf16[64,2048]{1,0:T(8,128)(2,1)S(1)}, u32[]{:S(2)}, u32[]{:S(2)}) collective-permute-start(bf16[64,2048]{1,0:T(8,128)(2,1)S(1)} %collective-permute-done.24.refs_1_), channel_id=1, source_target_pairs={{0,1},{1,0},{2,3},{3,2},{4,5},{5,4},{6,7},{7,6},{8,9},{9,8},{10,11... | collective-permute-start | bytes 786440 | tf_op jit(solution)/shard_map/ppermute | solution.py:500
  153.6 6.4 %collective-permute-start.35 = (bf16[64,1024]{1,0:T(8,128)(2,1)S(1)}, bf16[64,1024]{1,0:T(8,128)(2,1)S(1)}, u32[]{:S(2)}, u32[]{:S(2)}) collective-permute-start(bf16[64,1024]{1,0:T(8,128)(2,1)S(1)} %get-tuple-element.121), channel_id=1, source_target_pairs={{0,2},{1,3},{2,0},{3,1},{4,6},{5,7},{6,4},{7,5},{8,10},{9,11},{10,... | collective-permute-start | bytes 393224 | tf_op jit(solution)/shard_map/ppermute | solution.py:504
  153.9 8.8 %collective-permute-start.32 = (bf16[64,1024]{1,0:T(8,128)(2,1)S(1)}, bf16[64,1024]{1,0:T(8,128)(2,1)S(1)}, u32[]{:S(2)}, u32[]{:S(2)}) collective-permute-start(bf16[64,1024]{1,0:T(8,128)(2,1)S(1)} %get-tuple-element.116), channel_id=1, source_target_pairs={{0,2},{1,3},{2,0},{3,1},{4,6},{5,7},{6,4},{7,5},{8,10},{9,11},{10,... | collective-permute-start | bytes 393224 | tf_op jit(solution)/shard_map/ppermute | solution.py:504
  160.0 11.8 %collective-permute-start.36 = (bf16[64,1024]{1,0:T(8,128)(2,1)S(1)}, bf16[64,1024]{1,0:T(8,128)(2,1)S(1)}, u32[]{:S(2)}, u32[]{:S(2)}) collective-permute-start(bf16[64,1024]{1,0:T(8,128)(2,1)S(1)} %add_convert_fusion), channel_id=1, source_target_pairs={{0,4},{1,5},{2,6},{3,7},{4,0},{5,1},{6,2},{7,3},{8,12},{9,13},{10,... | collective-permute-start | bytes 393224 | tf_op jit(solution)/shard_map/ppermute | solution.py:504
  160.2 11.6 %collective-permute-start.37 = (bf16[64,1024]{1,0:T(8,128)(2,1)S(1)}, bf16[64,1024]{1,0:T(8,128)(2,1)S(1)}, u32[]{:S(2)}, u32[]{:S(2)}) collective-permute-start(bf16[64,1024]{1,0:T(8,128)(2,1)S(1)} %get-tuple-element.123), channel_id=1, source_target_pairs={{0,2},{1,3},{2,0},{3,1},{4,6},{5,7},{6,4},{7,5},{8,10},{9,11},{10,... | collective-permute-start | bytes 393224 | tf_op jit(solution)/shard_map/ppermute | solution.py:504
  162.8 10.5 %collective-permute-start.34 = (bf16[64,1024]{1,0:T(8,128)(2,1)S(1)}, bf16[64,1024]{1,0:T(8,128)(2,1)S(1)}, u32[]{:S(2)}, u32[]{:S(2)}) collective-permute-start(bf16[64,1024]{1,0:T(8,128)(2,1)S(1)} %get-tuple-element.118), channel_id=1, source_target_pairs={{0,2},{1,3},{2,0},{3,1},{4,6},{5,7},{6,4},{7,5},{8,10},{9,11},{10,... | collective-permute-start | bytes 393224 | tf_op jit(solution)/shard_map/ppermute | solution.py:504
  163.1 10.1 %collective-permute-start.33 = (bf16[64,1024]{1,0:T(8,128)(2,1)S(1)}, bf16[64,1024]{1,0:T(8,128)(2,1)S(1)}, u32[]{:S(2)}, u32[]{:S(2)}) collective-permute-start(bf16[64,1024]{1,0:T(8,128)(2,1)S(1)} %add_convert_fusion.1), channel_id=1, source_target_pairs={{0,4},{1,5},{2,6},{3,7},{4,0},{5,1},{6,2},{7,3},{8,12},{9,13},{10,... | collective-permute-start | bytes 393224 | tf_op jit(solution)/shard_map/ppermute | solution.py:504
  (48 other events, 319.2 us)
